TPU v7x, 128 devices: a whole 4x4x4 slice. The times are simulated.
128 devices in a mesh: fsdp: 16 (over y_hi, x, core), seq: 8 (over y_lo, z).
Axes of the slice: x: 4, y: 4 (y_hi: 2, y_lo: 2; y = y_hi * 2 + y_lo), z: 4, core: 2. Of those that a mesh axis runs over, the one named last changes fastest.
Arguments:
- tokens: bfloat16 [16, 2048, 1024], P('fsdp', 'seq'), may hold values from -6 to 6
- encoded: bfloat16 [16, 1024, 1024], P('fsdp', 'seq'), may hold values from -6 to 6
- unit_ids: int32 [16, 2048], P('fsdp', 'seq'), may hold values from 0 to 15, as said below
- text_ids: int32 [16, 1024], P('fsdp', 'seq'), may hold values from 0 to 15, as said below
- cotangent: bfloat16 [16, 2048, 1024], P('fsdp', 'seq'), may hold values from -6 to 6
- attn_in: float32 [6, 1024, 1024], P(None, ('fsdp', 'seq')), may hold values from -0.1875 to 0.1875
- attn_out: float32 [2, 1024, 1024], P(None, ('fsdp', 'seq')), may hold values from -0.75 to 0.75
- w_up: float32 [1024, 4096], P(('fsdp', 'seq')), may hold values from -0.1875 to 0.1875
- w_down: float32 [4096, 1024], P(('fsdp', 'seq')), may hold values from -0.09375 to 0.09375
- norm_gains: float32 [4, 1024], P(None, ('fsdp', 'seq')), may hold values from 0.25 to 1.75
- shifts: float32 [4, 1024], P(None, ('fsdp', 'seq')), may hold values from -1.8 to 1.8
- biases: float32 [7, 1024], P(None, ('fsdp', 'seq')), may hold values from -1.8 to 1.8
- up_bias: float32 [4096], P(('fsdp', 'seq')), may hold values from -1.8 to 1.8
Outputs:
- layer_out: float32 [16, 2048, 1024], P('fsdp', 'seq')
- d_tokens: float32 [16, 2048, 1024], P('fsdp', 'seq')
- d_encoded: float32 [16, 1024, 1024], P('fsdp', 'seq')
- d_attn_in: float32 [6, 1024, 1024], P(None, ('fsdp', 'seq'))
- d_attn_out: float32 [2, 1024, 1024], P(None, ('fsdp', 'seq'))
- d_w_up: float32 [1024, 4096], P(('fsdp', 'seq'))
- d_w_down: float32 [4096, 1024], P(('fsdp', 'seq'))
- d_norm_gains: float32 [4, 1024], P(None, ('fsdp', 'seq'))
- d_shifts: float32 [4, 1024], P(None, ('fsdp', 'seq'))
- d_biases: float32 [7, 1024], P(None, ('fsdp', 'seq'))
- d_up_bias: float32 [4096], P(('fsdp', 'seq'))
Inputs may be any that keep to these rules, and one draw needn't show every extreme that they name: `unit_ids`: along a sequence the ids never fall, and each of the 16 documents has one unit token or more. `text_ids`: along a sequence the ids never fall, and each of the 16 documents has one text token or more; the unit tokens of a document attend to the text tokens with the same id in the same sequence.
All inputs are finite; a program needn't handle non-finite values.
Results may differ from a plain program's by a relative error of at most 0.025.
Values may be sent and summed in bfloat16 or wider, within the bound.
No kernel may reach another device: no remote copies, remote signals or barrier semaphores. Data moves between devices by JAX's collectives and lax.ppermute only.
A program may use at most 256 MiB of HBM per device.

v0:
```python
import math

import jax
import jax.numpy as jnp
from jax import lax
from jax.sharding import PartitionSpec as P

HEADS = 16
HEAD_DIM = 64


norm_eps = 1e-05
masked_score = -1e30


def norm_forward(values, gain_row, shift_row):
    row_mean = jnp.mean(values, axis=-1, keepdims=True)
    centered = values - row_mean
    spread = jnp.mean(centered * centered, axis=-1, keepdims=True)
    inverse = lax.rsqrt(spread + norm_eps)
    normed = centered * inverse
    return (normed * gain_row + shift_row, normed, inverse)


def norm_backward(upstream, normed, inverse, gain_row):
    scaled = upstream * gain_row
    inner_part = (
        scaled
        - jnp.mean(scaled, axis=-1, keepdims=True)
        - normed * jnp.mean(scaled * normed, axis=-1, keepdims=True)
    )
    return (inverse * inner_part, jnp.sum(upstream * normed, axis=0), jnp.sum(upstream, axis=0))


def split_groups(matrix):
    return matrix.reshape(matrix.shape[0], HEADS // 4, 4 * HEAD_DIM).transpose(1, 0, 2)


def join_groups(stacked):
    return stacked.transpose(1, 0, 2).reshape(stacked.shape[1], stacked.shape[0] * stacked.shape[2])


def group_scores(q_group, k_group, allowed):
    q_heads = q_group.reshape(q_group.shape[0], 4, HEAD_DIM)
    k_heads = k_group.reshape(k_group.shape[0], 4, HEAD_DIM)
    scores = jnp.einsum("qhd,khd->hqk", q_heads, k_heads, preferred_element_type=jnp.float32) * (
        1.0 / math.sqrt(HEAD_DIM)
    )
    return (jnp.where(allowed[None], scores, masked_score), q_heads, k_heads)


def attend_forward(queries, key_rows, value_rows, allowed):

    def one_group(pieces):
        scores, q_heads, k_heads = group_scores(pieces[0], pieces[1], allowed)
        v_heads = pieces[2].reshape(pieces[2].shape[0], 4, HEAD_DIM)
        row_max = jnp.max(scores, axis=-1, keepdims=True)
        weights = jnp.exp(scores - row_max)
        row_sum = jnp.sum(weights, axis=-1, keepdims=True)
        probs_low = (weights / row_sum).astype(jnp.bfloat16)
        mixed_rows = jnp.einsum(
            "hqk,khd->qhd", probs_low, v_heads, preferred_element_type=jnp.float32
        )
        return (
            mixed_rows.reshape(mixed_rows.shape[0], 4 * HEAD_DIM),
            row_max[..., 0] + jnp.log(row_sum[..., 0]),
        )

    mixed_rows, log_sums = lax.map(
        one_group, (split_groups(queries), split_groups(key_rows), split_groups(value_rows))
    )
    return (join_groups(mixed_rows), log_sums)


def attend_backward(queries, key_rows, value_rows, grad_rows, log_sums, allowed):
    score_scale = 1.0 / math.sqrt(HEAD_DIM)

    def one_group(pieces):
        scores, q_heads, k_heads = group_scores(pieces[0], pieces[1], allowed)
        v_heads = pieces[2].reshape(pieces[2].shape[0], 4, HEAD_DIM)
        g_heads = pieces[3].reshape(pieces[3].shape[0], 4, HEAD_DIM)
        probs_full = jnp.exp(scores - pieces[4][..., None])
        d_values = jnp.einsum(
            "hqk,qhd->khd",
            probs_full.astype(jnp.bfloat16),
            g_heads,
            preferred_element_type=jnp.float32,
        )
        d_probs = jnp.einsum("qhd,khd->hqk", g_heads, v_heads, preferred_element_type=jnp.float32)
        inner_sum = jnp.sum(probs_full * d_probs, axis=-1, keepdims=True)
        d_scores = (probs_full * (d_probs - inner_sum)).astype(jnp.bfloat16)
        d_queries = (
            jnp.einsum("hqk,khd->qhd", d_scores, k_heads, preferred_element_type=jnp.float32)
            * score_scale
        )
        d_keys = (
            jnp.einsum("hqk,qhd->khd", d_scores, q_heads, preferred_element_type=jnp.float32)
            * score_scale
        )
        group_width = 4 * HEAD_DIM
        return (
            d_queries.reshape(-1, group_width),
            d_keys.reshape(-1, group_width),
            d_values.reshape(-1, group_width),
        )

    grad_q, grad_k, grad_v = lax.map(
        one_group,
        (
            split_groups(queries),
            split_groups(key_rows),
            split_groups(value_rows),
            split_groups(grad_rows),
            log_sums,
        ),
    )
    return (join_groups(grad_q), join_groups(grad_k), join_groups(grad_v))


def local(
    tokens,
    encoded,
    unit_ids,
    text_ids,
    cotangent,
    attn_in,
    attn_out,
    w_up,
    w_down,
    norm_gains,
    shifts,
    biases,
    up_bias,
):
    seq_index = lax.axis_index("seq")
    row_count = tokens.shape[1]
    inputs32 = tokens[0].astype(jnp.float32)
    enc_rows = encoded[0]
    own_units = unit_ids[0]
    own_text = text_ids[0]
    self_in = attn_in[0:3].astype(jnp.bfloat16)
    self_out = attn_out[0].astype(jnp.bfloat16)
    self_small = jnp.concatenate([norm_gains[0:1], shifts[0:1], biases[0:3]], axis=0).astype(
        jnp.bfloat16
    )
    cross_in = attn_in[3:6].astype(jnp.bfloat16)
    cross_out = attn_out[1].astype(jnp.bfloat16)
    cross_small = jnp.concatenate([norm_gains[1:2], shifts[1:2], biases[3:6]], axis=0).astype(
        jnp.bfloat16
    )
    up_local = w_up.astype(jnp.bfloat16)
    down_local = w_down.astype(jnp.bfloat16)
    ffn_small = jnp.concatenate(
        [norm_gains[2:3], shifts[2:3], norm_gains[3:4], shifts[3:4], biases[6:7]], axis=0
    ).astype(jnp.bfloat16)
    up_shift = up_bias.astype(jnp.bfloat16)
    self_proj, self_mix, self_params = (
        lax.all_gather(self_in, ("fsdp", "seq"), axis=1, tiled=True),
        lax.all_gather(self_out, ("fsdp", "seq"), axis=0, tiled=True),
        lax.all_gather(self_small, ("fsdp", "seq"), axis=1, tiled=True),
    )
    self_vec = self_params.astype(jnp.float32)
    normed_in, normed_one, inverse_one = norm_forward(inputs32, self_vec[0], self_vec[1])
    act_one = normed_in.astype(jnp.bfloat16)
    triple = jnp.einsum("td,kde->kte", act_one, self_proj, preferred_element_type=jnp.float32)
    queries = (triple[0] + self_vec[2]).astype(jnp.bfloat16)
    key_local = triple[1].astype(jnp.bfloat16)
    value_local = (triple[2] + self_vec[3]).astype(jnp.bfloat16)
    key_rows, value_rows, key_ids = (
        lax.all_gather(key_local, "seq", axis=0, tiled=True),
        lax.all_gather(value_local, "seq", axis=0, tiled=True),
        lax.all_gather(own_units, "seq", axis=0, tiled=True),
    )
    query_pos = seq_index * row_count + jnp.arange(row_count, dtype=jnp.int32)
    key_pos = jnp.arange(key_rows.shape[0], dtype=jnp.int32)
    self_mask = (own_units[:, None] == key_ids[None, :]) & (query_pos[:, None] >= key_pos[None, :])
    mixed_self, sums_self = attend_forward(queries, key_rows, value_rows, self_mask)
    mixed_self = mixed_self.astype(jnp.bfloat16)
    after_self = (
        inputs32 + jnp.dot(mixed_self, self_mix, preferred_element_type=jnp.float32) + self_vec[4]
    )
    cross_proj, cross_mix, cross_params = (
        lax.all_gather(cross_in, ("fsdp", "seq"), axis=1, tiled=True),
        lax.all_gather(cross_out, ("fsdp", "seq"), axis=0, tiled=True),
        lax.all_gather(cross_small, ("fsdp", "seq"), axis=1, tiled=True),
    )
    cross_vec = cross_params.astype(jnp.float32)
    normed_mid, normed_two, inverse_two = norm_forward(after_self, cross_vec[0], cross_vec[1])
    act_two = normed_mid.astype(jnp.bfloat16)
    queries_two = (
        jnp.dot(act_two, cross_proj[0], preferred_element_type=jnp.float32) + cross_vec[2]
    ).astype(jnp.bfloat16)
    text_pair = jnp.einsum(
        "td,kde->kte", enc_rows, cross_proj[1:3], preferred_element_type=jnp.float32
    )
    text_key_local = text_pair[0].astype(jnp.bfloat16)
    text_value_local = (text_pair[1] + cross_vec[3]).astype(jnp.bfloat16)
    text_keys, text_values, text_key_ids = (
        lax.all_gather(text_key_local, "seq", axis=0, tiled=True),
        lax.all_gather(text_value_local, "seq", axis=0, tiled=True),
        lax.all_gather(own_text, "seq", axis=0, tiled=True),
    )
    cross_mask = own_units[:, None] == text_key_ids[None, :]
    mixed_cross, sums_cross = attend_forward(queries_two, text_keys, text_values, cross_mask)
    mixed_cross = mixed_cross.astype(jnp.bfloat16)
    after_cross = (
        after_self
        + jnp.dot(mixed_cross, cross_mix, preferred_element_type=jnp.float32)
        + cross_vec[4]
    )
    ffn_up, ffn_down, ffn_params, ffn_shift = (
        lax.all_gather(up_local, ("fsdp", "seq"), axis=0, tiled=True),
        lax.all_gather(down_local, ("fsdp", "seq"), axis=0, tiled=True),
        lax.all_gather(ffn_small, ("fsdp", "seq"), axis=1, tiled=True),
        lax.all_gather(up_shift, ("fsdp", "seq"), axis=0, tiled=True),
    )
    ffn_vec = ffn_params.astype(jnp.float32)
    normed_ffn, normed_three, inverse_three = norm_forward(after_cross, ffn_vec[0], ffn_vec[1])
    act_three = normed_ffn.astype(jnp.bfloat16)
    before_act = jnp.dot(act_three, ffn_up, preferred_element_type=jnp.float32) + ffn_shift.astype(
        jnp.float32
    )
    sigma_act = jax.nn.sigmoid(before_act)
    hidden = (before_act * sigma_act).astype(jnp.bfloat16)
    after_ffn = (
        after_cross + jnp.dot(hidden, ffn_down, preferred_element_type=jnp.float32) + ffn_vec[4]
    )
    layer_result, normed_four, inverse_four = norm_forward(after_ffn, ffn_vec[2], ffn_vec[3])
    back_up, back_down, back_ffn = (
        lax.all_gather(up_local, ("fsdp", "seq"), axis=0, tiled=True),
        lax.all_gather(down_local, ("fsdp", "seq"), axis=0, tiled=True),
        lax.all_gather(ffn_small, ("fsdp", "seq"), axis=1, tiled=True),
    )
    back_ffn_vec = back_ffn.astype(jnp.float32)
    grad_output = cotangent[0].astype(jnp.float32)
    grad_ffn, grad_gain_four, grad_shift_four = norm_backward(
        grad_output, normed_four, inverse_four, back_ffn_vec[2]
    )
    grad_bias_down = jnp.sum(grad_ffn, axis=0)
    grad_ffn_low = grad_ffn.astype(jnp.bfloat16)
    grad_down = jnp.einsum("tf,td->fd", hidden, grad_ffn_low, preferred_element_type=jnp.float32)
    grad_hidden = jnp.einsum(
        "td,fd->tf", grad_ffn_low, back_down, preferred_element_type=jnp.float32
    )
    grad_before = grad_hidden * sigma_act * (1.0 + before_act * (1.0 - sigma_act))
    grad_up_shift = jnp.sum(grad_before, axis=0)
    grad_before_low = grad_before.astype(jnp.bfloat16)
    grad_up = jnp.einsum(
        "td,tf->df", act_three, grad_before_low, preferred_element_type=jnp.float32
    )
    grad_act_three = jnp.einsum(
        "tf,df->td", grad_before_low, back_up, preferred_element_type=jnp.float32
    )
    back_three, grad_gain_three, grad_shift_three = norm_backward(
        grad_act_three, normed_three, inverse_three, back_ffn_vec[0]
    )
    grad_after_cross = grad_ffn + back_three
    ffn_small_grad = jnp.stack(
        [grad_gain_three, grad_shift_three, grad_gain_four, grad_shift_four, grad_bias_down]
    )
    ffn_owned = (
        lax.psum_scatter(grad_up, ("fsdp", "seq"), scatter_dimension=0, tiled=True),
        lax.psum_scatter(grad_down, ("fsdp", "seq"), scatter_dimension=0, tiled=True),
        lax.psum_scatter(ffn_small_grad, ("fsdp", "seq"), scatter_dimension=1, tiled=True),
        lax.psum_scatter(grad_up_shift, ("fsdp", "seq"), scatter_dimension=0, tiled=True),
    )
    back_cross_proj, back_cross_mix, back_cross = (
        lax.all_gather(cross_in, ("fsdp", "seq"), axis=1, tiled=True),
        lax.all_gather(cross_out, ("fsdp", "seq"), axis=0, tiled=True),
        lax.all_gather(cross_small, ("fsdp", "seq"), axis=1, tiled=True),
    )
    back_cross_vec = back_cross.astype(jnp.float32)
    grad_bias_cross = jnp.sum(grad_after_cross, axis=0)
    grad_cross_low = grad_after_cross.astype(jnp.bfloat16)
    grad_cross_mix = jnp.einsum(
        "tc,td->cd", mixed_cross, grad_cross_low, preferred_element_type=jnp.float32
    )
    grad_mixed_cross = jnp.einsum(
        "td,cd->tc", grad_cross_low, back_cross_mix, preferred_element_type=jnp.float32
    ).astype(jnp.bfloat16)
    grad_q_two, grad_k_all, grad_v_all = attend_backward(
        queries_two, text_keys, text_values, grad_mixed_cross, sums_cross, cross_mask
    )
    grad_k_text, grad_v_text = (
        lax.psum_scatter(
            grad_k_all.astype(jnp.bfloat16), "seq", scatter_dimension=0, tiled=True
        ).astype(jnp.float32),
        lax.psum_scatter(
            grad_v_all.astype(jnp.bfloat16), "seq", scatter_dimension=0, tiled=True
        ).astype(jnp.float32),
    )
    grad_bias_q_two = jnp.sum(grad_q_two, axis=0)
    grad_bias_v_two = jnp.sum(grad_v_text, axis=0)
    grad_q_two_low = grad_q_two.astype(jnp.bfloat16)
    grad_text_low = jnp.stack([grad_k_text, grad_v_text]).astype(jnp.bfloat16)
    grad_cross_q = jnp.einsum(
        "td,te->de", act_two, grad_q_two_low, preferred_element_type=jnp.float32
    )
    grad_cross_kv = jnp.einsum(
        "td,kte->kde", enc_rows, grad_text_low, preferred_element_type=jnp.float32
    )
    grad_encoded = jnp.einsum(
        "kte,kde->td", grad_text_low, back_cross_proj[1:3], preferred_element_type=jnp.float32
    )
    grad_act_two = jnp.einsum(
        "te,de->td", grad_q_two_low, back_cross_proj[0], preferred_element_type=jnp.float32
    )
    back_two, grad_gain_two, grad_shift_two = norm_backward(
        grad_act_two, normed_two, inverse_two, back_cross_vec[0]
    )
    grad_after_self = grad_after_cross + back_two
    cross_proj_grad = jnp.concatenate([grad_cross_q[None], grad_cross_kv], axis=0)
    cross_small_grad = jnp.stack(
        [grad_gain_two, grad_shift_two, grad_bias_q_two, grad_bias_v_two, grad_bias_cross]
    )
    cross_owned = (
        lax.psum_scatter(cross_proj_grad, ("fsdp", "seq"), scatter_dimension=1, tiled=True),
        lax.psum_scatter(grad_cross_mix, ("fsdp", "seq"), scatter_dimension=0, tiled=True),
        lax.psum_scatter(cross_small_grad, ("fsdp", "seq"), scatter_dimension=1, tiled=True),
    )
    back_self_proj, back_self_mix, back_self = (
        lax.all_gather(self_in, ("fsdp", "seq"), axis=1, tiled=True),
        lax.all_gather(self_out, ("fsdp", "seq"), axis=0, tiled=True),
        lax.all_gather(self_small, ("fsdp", "seq"), axis=1, tiled=True),
    )
    back_self_vec = back_self.astype(jnp.float32)
    grad_bias_self = jnp.sum(grad_after_self, axis=0)
    grad_self_low = grad_after_self.astype(jnp.bfloat16)
    grad_self_mix = jnp.einsum(
        "tc,td->cd", mixed_self, grad_self_low, preferred_element_type=jnp.float32
    )
    grad_mixed_self = jnp.einsum(
        "td,cd->tc", grad_self_low, back_self_mix, preferred_element_type=jnp.float32
    ).astype(jnp.bfloat16)
    grad_q_one, grad_k_seq, grad_v_seq = attend_backward(
        queries, key_rows, value_rows, grad_mixed_self, sums_self, self_mask
    )
    grad_k_own, grad_v_own = (
        lax.psum_scatter(
            grad_k_seq.astype(jnp.bfloat16), "seq", scatter_dimension=0, tiled=True
        ).astype(jnp.float32),
        lax.psum_scatter(
            grad_v_seq.astype(jnp.bfloat16), "seq", scatter_dimension=0, tiled=True
        ).astype(jnp.float32),
    )
    grad_bias_q_one = jnp.sum(grad_q_one, axis=0)
    grad_bias_v_one = jnp.sum(grad_v_own, axis=0)
    grad_triple_low = jnp.stack([grad_q_one, grad_k_own, grad_v_own]).astype(jnp.bfloat16)
    self_proj_grad = jnp.einsum(
        "td,kte->kde", act_one, grad_triple_low, preferred_element_type=jnp.float32
    )
    grad_act_one = jnp.einsum(
        "kte,kde->td", grad_triple_low, back_self_proj, preferred_element_type=jnp.float32
    )
    back_one, grad_gain_one, grad_shift_one = norm_backward(
        grad_act_one, normed_one, inverse_one, back_self_vec[0]
    )
    grad_tokens = grad_after_self + back_one
    self_small_grad = jnp.stack(
        [grad_gain_one, grad_shift_one, grad_bias_q_one, grad_bias_v_one, grad_bias_self]
    )
    self_owned = (
        lax.psum_scatter(self_proj_grad, ("fsdp", "seq"), scatter_dimension=1, tiled=True),
        lax.psum_scatter(grad_self_mix, ("fsdp", "seq"), scatter_dimension=0, tiled=True),
        lax.psum_scatter(self_small_grad, ("fsdp", "seq"), scatter_dimension=1, tiled=True),
    )
    owned_grads = tuple(self_owned) + tuple(cross_owned) + tuple(ffn_owned)
    grad_attn_in = jnp.concatenate([owned_grads[0], owned_grads[3]], axis=0)
    grad_attn_out = jnp.stack([owned_grads[1], owned_grads[4]])
    self_part = owned_grads[2]
    cross_part = owned_grads[5]
    ffn_part = owned_grads[8]
    grad_gains = jnp.stack([self_part[0], cross_part[0], ffn_part[0], ffn_part[2]])
    grad_shifts = jnp.stack([self_part[1], cross_part[1], ffn_part[1], ffn_part[3]])
    grad_biases = jnp.concatenate([self_part[2:5], cross_part[2:5], ffn_part[4:5]], axis=0)
    return (
        layer_result[None],
        grad_tokens[None],
        grad_encoded[None],
        grad_attn_in,
        grad_attn_out,
        owned_grads[6],
        owned_grads[7],
        grad_gains,
        grad_shifts,
        grad_biases,
        owned_grads[9],
    )


def solution(mesh):
    placed = (
        P("fsdp", "seq", None),
        P("fsdp", "seq", None),
        P("fsdp", "seq"),
        P("fsdp", "seq"),
        P("fsdp", "seq", None),
        P(None, ("fsdp", "seq"), None),
        P(None, ("fsdp", "seq"), None),
        P(("fsdp", "seq"), None),
        P(("fsdp", "seq"), None),
        P(None, ("fsdp", "seq")),
        P(None, ("fsdp", "seq")),
        P(None, ("fsdp", "seq")),
        P(("fsdp", "seq")),
    )
    return jax.shard_map(
        local,
        mesh=mesh,
        in_specs=placed,
        out_specs=(
            P("fsdp", "seq", None),
            P("fsdp", "seq", None),
            P("fsdp", "seq", None),
            P(None, ("fsdp", "seq"), None),
            P(None, ("fsdp", "seq"), None),
            P(("fsdp", "seq"), None),
            P(("fsdp", "seq"), None),
            P(None, ("fsdp", "seq")),
            P(None, ("fsdp", "seq")),
            P(None, ("fsdp", "seq")),
            P(("fsdp", "seq")),
        ),
        check_vma=False,
    )
```

profile of v0, /device:TPU:0, one launch (start us, length us, event | category | flops | bytes accessed | tf_op | source)
XLA Modules:
  0.0 5433.0 jit_solution(1765198351761454347)
XLA Ops:
  12.3 319.4 %all_gather.57 = bf16[5,1024]{0,1:T(8,128)(2,1)S(1)} all-gather(bf16[5,8]{0,1:T(8,128)(2,1)S(1)} %pad_maximum_fusion.10), channel_id=1, replica_groups=mesh['fsdp'=16,'seq'=8] {'fsdp','seq'}, dimensions={1}, use_global_device_ids=true | all-gather | bytes 10320 | tf_op jit(solution)/shard_map/all_gather | solution.py:160
  345.9 291.7 %all-gather.21.cloned.1.call-done = bf16[3,1024,1024]{2,1,0:T(8,128)(2,1)} async-done(((bf16[3,8,1024]{2,1,0:T(8,128)(2,1)}), bf16[3,1024,1024]{2,1,0:T(8,128)(2,1)}) %all-gather.21.cloned.1.call-update) | async-done | bytes 6291472 | tf_op jit(solution)/shard_map/all_gather | solution.py:183
  642.1 319.4 %all_gather.64 = bf16[5,1024]{0,1:T(8,128)(2,1)S(1)} all-gather(bf16[5,8]{0,1:T(8,128)(2,1)S(1)} %pad_maximum_fusion.11), channel_id=1, replica_groups=mesh['fsdp'=16,'seq'=8] {'fsdp','seq'}, dimensions={1}, use_global_device_ids=true | all-gather | bytes 10320 | tf_op jit(solution)/shard_map/all_gather | solution.py:185
  966.3 15.0 all-gather.3
  981.3 17.1 all-gather
  998.6 62.6 %all-reduce = bf16[4096]{0:T(1024)(128)(2,1)S(1)} all-reduce(bf16[4096]{0:T(1024)(128)(2,1)S(1)} %dynamic-update-slice), channel_id=1, replica_groups=mesh['fsdp'=16,'seq'=8] {'fsdp','seq'}, use_global_device_ids=true, to_apply=%add | all-reduce | flops 4096 | bytes 16384
  1061.2 312.9 %all_gather.69 = bf16[5,1024]{0,1:T(8,128)(2,1)S(1)} all-gather(bf16[5,8]{0,1:T(8,128)(2,1)S(1)} %concatenate.23), channel_id=1, replica_groups=mesh['fsdp'=16,'seq'=8] {'fsdp','seq'}, dimensions={1}, use_global_device_ids=true | all-gather | bytes 10320 | tf_op jit(solution)/shard_map/all_gather | solution.py:214
  1380.0 6.7 copy.87
  1386.7 6.5 copy.89
  1393.2 37.3 while.56
  1437.3 25.4 while.57
  1465.6 297.5 %all-gather.25.cloned.1.call-done = bf16[1024,4096]{1,0:T(8,128)(2,1)} async-done(((bf16[8,4096]{1,0:T(8,128)(2,1)}), bf16[1024,4096]{1,0:T(8,128)(2,1)}) %all-gather.25.cloned.1.call-update) | async-done | bytes 8388624 | tf_op jit(solution)/shard_map/all_gather | solution.py:212
  1763.1 7.8 convolution_add_fusion
  1770.9 306.8 %all-gather.27.cloned.1.call-done = bf16[4096,1024]{1,0:T(8,128)(2,1)} async-done(((bf16[32,1024]{1,0:T(8,128)(2,1)}), bf16[4096,1024]{1,0:T(8,128)(2,1)}) %all-gather.27.cloned.1.call-update) | async-done | bytes 8388624 | tf_op jit(solution)/shard_map/all_gather | solution.py:213
  2077.7 7.2 fusion.136
  2088.2 7.7 fusion.137
  2104.0 49.2 while.58
  2170.7 80.6 %while.59 = (s32[]{:T(128)}, f32[4,256,256]{1,2,0:T(8,128)}, bf16[4,2048,256]{1,2,0:T(8,128)(2,1)}, bf16[4,2048,256]{1,2,0:T(8,128)(2,1)}, bf16[4,2048,256]{1,2,...) while((s32[]{:T(128)}, f32[4,256,256]{1,2,0:T(8,128)}, ...), condition=%wide.region_27.28_spmd.clone, body=%wide.region_25.27_spmd.clone.sunk | while | flops 1376320512 | bytes 80517280 | solution.py:107
  2257.8 6.4 copy.94
  2288.1 12.0 pad_maximum_fusion
  2300.2 18.6 copy.81
  2320.6 45.9 reduce-scatter.12.cloned.1.call-done
  2373.5 7.6 convolution_bitcast_fusion
  2381.0 18.4 copy.78
  2400.6 10.5 fusion.112
  2412.4 9.9 fusion.96
  2427.7 583.1 %reduce-scatter.22.cloned.1.call-done = f32[8,1024]{1,0:T(8,128)} async-done(((f32[1024,1024]{1,0:T(8,128)}), f32[8,1024]{1,0:T(8,128)}) %reduce-scatter.22.cloned.1.call-update) | async-done | bytes 32784 | tf_op jit(solution)/shard_map/reduce_scatter | solution.py:318
  3010.8 641.3 %reduce-scatter.20.cloned.1.call-done = f32[8,1024]{1,0:T(8,128)} async-done(((f32[1024,1024]{1,0:T(8,128)}), f32[8,1024]{1,0:T(8,128)}) %reduce-scatter.20.cloned.1.call-update) | async-done | bytes 32784 | tf_op jit(solution)/shard_map/reduce_scatter | solution.py:364
  3654.8 136.1 %all-reduce.12.cloned.1.call-done = (f32[5,1024]{1,0:T(8,128)}, f32[5,1024]{1,0:T(8,128)}, f32[5,1024]{1,0:T(8,128)}, f32[4096]{0:T(1024)}) async-done(((f32[5,1024]{1,0:T(8,128)}, f32[5,1024]{1,0:T(8,128)}, f32[5,1024]{1,0:T(8,128)}, f32[4096]{0:T(1024)}), (f32[5,1024]{1,0:T(8,128)}, f32[5,1024]{1,0:T(8,128)}, f32[5,1024]{1,0:T(8,128)}, f32[4096]{0:T(1024)})) %all-reduce.12.cloned.1.call-update) | async-done | bytes 77840
  3796.3 289.6 %all-reduce.14.cloned.1.call-done = (f32[3,1024,1024]{2,0,1:T(4,128)}, f32[3,1024,1024]{2,0,1:T(4,128)}) async-done(((f32[3,1024,1024]{2,0,1:T(4,128)}, f32[3,1024,1024]{2,0,1:T(4,128)}), (f32[3,1024,1024]{2,0,1:T(4,128)}, f32[3,1024,1024]{2,0,1:T(4,128)})) %all-reduce.14.cloned.1.call-update) | async-done | bytes 25165840
  4088.5 668.8 %reduce-scatter.26.cloned.1.call-done = f32[32,1024]{1,0:T(8,128)} async-done(((f32[4096,1024]{1,0:T(8,128)}), f32[32,1024]{1,0:T(8,128)}) %reduce-scatter.26.cloned.1.call-update) | async-done | bytes 131088 | tf_op jit(solution)/shard_map/reduce_scatter | solution.py:263
  4757.4 668.4 %reduce-scatter.24.cloned.1.call-done = f32[8,4096]{1,0:T(8,128)} async-done(((f32[1024,4096]{1,0:T(8,128)}), f32[8,4096]{1,0:T(8,128)}) %reduce-scatter.24.cloned.1.call-update) | async-done | bytes 131088 | tf_op jit(solution)/shard_map/reduce_scatter | solution.py:262
  (495 shorter events, 321.3 us)
Async XLA Ops:
  7.2 630.5 %copy-start = (bf16[1,128,1024]{2,1,0:T(8,128)(2,1)S(1)}, bf16[1,128,1024]{2,1,0:T(8,128)(2,1)}, u32[]{:S(2)}) copy-start(bf16[1,128,1024]{2,1,0:T(8,128)(2,1)} %param.22) | copy-start | bytes 786436
  7.2 328.4 %all-gather.17.cloned.1.call-start = ((), (), s32[]{:S(2)}) async-start(), calls=%async_computation.8 | async-start | bytes 6340608 | tf_op jit(solution)/shard_map/all_gather | solution.py:158
  8.9 628.8 %all-gather.21.cloned.1.call-start = ((), (), s32[]{:S(2)}) async-start(), calls=%async_computation.10 | async-start | bytes 6340608 | tf_op jit(solution)/shard_map/all_gather | solution.py:183
  9.7 1370.3 %all-gather.19.cloned.1.call-start = ((), (), s32[]{:S(2)}) async-start(), calls=%async_computation.9 | async-start | bytes 4718592 | tf_op jit(solution)/shard_map/all_gather | solution.py:171
  343.0 1043.7 %all-gather.29.cloned.1.call-start = ((), (), s32[]{:S(2)}) async-start(), calls=%async_computation.22 | async-start | bytes 4718592 | tf_op jit(solution)/shard_map/all_gather | solution.py:170
  345.2 1085.4 %all-gather.31.cloned.1.call-start = ((), (), s32[]{:S(2)}) async-start(), calls=%async_computation.23 | async-start | bytes 2113536 | tf_op jit(solution)/shard_map/all_gather | solution.py:159
  345.9 618.8 %copy-start.31 = (f32[8,4096]{1,0:T(8,128)S(1)}, f32[8,4096]{1,0:T(8,128)}, u32[]{:S(2)}) copy-start(f32[8,4096]{1,0:T(8,128)} %param.28) | copy-start | bytes 393220
  345.9 1091.4 %all-gather.33.cloned.1.call-start = ((), (), s32[]{:S(2)}) async-start(), calls=%async_computation.24 | async-start | bytes 2359296 | tf_op jit(solution)/shard_map/all_gather | solution.py:199
  641.2 340.1 %copy-start.25 = (s32[1,256]{1,0:T(1,128)S(1)}, s32[1,256]{1,0:T(1,128)}, u32[]{:S(2)}) copy-start(s32[1,256]{1,0:T(1,128)} %param.23) | copy-start | bytes 3076
  642.0 795.3 %all-gather.23.cloned.1.call-start = ((), (), s32[]{:S(2)}) async-start(), calls=%async_computation.11 | async-start | bytes 2359296 | tf_op jit(solution)/shard_map/all_gather | solution.py:200
  962.9 471.0 %copy-start.40 = (f32[1024]{0:T(1024)}, f32[1024]{0:T(1024)S(1)}, u32[]{:S(2)}) copy-start(f32[1024]{0:T(1024)S(1)} %get-tuple-element.337) | copy-start | bytes 12292
  962.9 471.0 %copy-start.55 = (f32[1024]{0:T(1024)}, f32[1024]{0:T(1024)S(1)}, u32[]{:S(2)}) copy-start(f32[1024]{0:T(1024)S(1)} %get-tuple-element.336) | copy-start | bytes 12292
  963.8 498.9 %all-gather.35.cloned.1.call-start = ((), (), s32[]{:S(2)}) async-start(), calls=%async_computation.25 | async-start | bytes 2113536 | tf_op jit(solution)/shard_map/all_gather | solution.py:184
  964.6 798.5 %all-gather.25.cloned.1.call-start = ((), (), s32[]{:S(2)}) async-start(), calls=%async_computation.12 | async-start | bytes 8454144 | tf_op jit(solution)/shard_map/all_gather | solution.py:212
  965.3 1112.3 %all-gather.27.cloned.1.call-start = ((), (), s32[]{:S(2)}) async-start(), calls=%async_computation.13 | async-start | bytes 8454144 | tf_op jit(solution)/shard_map/all_gather | solution.py:213
  966.1 1316.5 %reduce-scatter.16.cloned.1.call-start = ((), (), s32[]{:S(2)}) async-start(), calls=%async_computation.16 | async-start | bytes 2359296 | tf_op jit(solution)/shard_map/reduce_scatter | solution.py:285
  1375.9 387.2 %copy-start.29 = (f32[1024]{0:T(1024)}, f32[1024]{0:T(1024)S(1)}, u32[]{:S(2)}) copy-start(f32[1024]{0:T(1024)S(1)} %get-tuple-element.332) | copy-start | bytes 12292
  1375.9 723.2 %copy-start.27 = (f32[1024]{0:T(1024)}, f32[1024]{0:T(1024)S(1)}, u32[]{:S(2)}) copy-start(f32[1024]{0:T(1024)S(1)} %get-tuple-element.333) | copy-start | bytes 12292
  1462.7 622.1 %copy-start.9 = (bf16[4,256,256]{1,2,0:T(8,128)(2,1)}, bf16[4,256,256]{1,2,0:T(8,128)(2,1)S(1)}, u32[]{:S(2)}) copy-start(bf16[4,256,256]{1,2,0:T(8,128)(2,1)S(1)} %get-tuple-element.196) | copy-start | bytes 1572868
  1465.3 633.8 %copy-start.1 = (f32[256,1024]{1,0:T(8,128)}, f32[256,1024]{1,0:T(8,128)S(1)}, u32[]{:S(2)}) copy-start(f32[256,1024]{1,0:T(8,128)S(1)} %get-tuple-element.481) | copy-start | bytes 3145732
  1465.3 633.8 %copy-start.42 = (f32[256]{0:T(256)}, f32[256]{0:T(256)S(1)}, u32[]{:S(2)}) copy-start(f32[256]{0:T(256)S(1)} %broadcast_multiply_fusion.9) | copy-start | bytes 3076
  1465.6 633.5 %copy-start.44 = (f32[256]{0:T(256)}, f32[256]{0:T(256)S(1)}, u32[]{:S(2)}) copy-start(f32[256]{0:T(256)S(1)} %add_rsqrt_fusion.1) | copy-start | bytes 3076
  2157.1 125.4 %reduce-scatter.18.cloned.1.call-start = ((), (), s32[]{:S(2)}) async-start(), calls=%async_computation.17 | async-start | bytes 2359296 | tf_op jit(solution)/shard_map/reduce_scatter | solution.py:288
  2169.5 150.0 %reduce-scatter.14.cloned.1.call-start = ((), (), s32[]{:S(2)}) async-start(), calls=%async_computation.15 | async-start | bytes 4718592 | tf_op jit(solution)/shard_map/reduce_scatter | solution.py:342
  2257.7 108.8 %reduce-scatter.12.cloned.1.call-start = ((), (), s32[]{:S(2)}) async-start(), calls=%async_computation.14 | async-start | bytes 4718592 | tf_op jit(solution)/shard_map/reduce_scatter | solution.py:339
  2264.2 746.6 %reduce-scatter.22.cloned.1.call-start = ((), (), s32[]{:S(2)}) async-start(), calls=%async_computation.19 | async-start | bytes 4227072 | tf_op jit(solution)/shard_map/reduce_scatter | solution.py:318
  2268.1 1384.0 %reduce-scatter.20.cloned.1.call-start = ((), (), s32[]{:S(2)}) async-start(), calls=%async_computation.18 | async-start | bytes 4227072 | tf_op jit(solution)/shard_map/reduce_scatter | solution.py:364
  2271.9 1519.0 %all-reduce.12.cloned.1.call-start = ((), (), s32[]{:S(2)}) async-start(), calls=%async_computation.26 | async-start | bytes 229376
  2373.4 1712.4 %all-reduce.14.cloned.1.call-start = ((), (), s32[]{:S(2)}) async-start(), calls=%async_computation.27 | async-start | bytes 67108864
  2399.4 2358.0 %reduce-scatter.26.cloned.1.call-start = ((), (), s32[]{:S(2)}) async-start(), calls=%async_computation.21 | async-start | bytes 16908288 | tf_op jit(solution)/shard_map/reduce_scatter | solution.py:263
  2411.2 3014.6 %reduce-scatter.24.cloned.1.call-start = ((), (), s32[]{:S(2)}) async-start(), calls=%async_computation.20 | async-start | bytes 16908288 | tf_op jit(solution)/shard_map/reduce_scatter | solution.py:262
  2422.3 1231.2 %copy-start.21 = (f32[256,1024]{1,0:T(8,128)S(1)}, f32[256,1024]{1,0:T(8,128)}, u32[]{:S(2)}) copy-start(f32[256,1024]{1,0:T(8,128)} %get-tuple-element.486) | copy-start | bytes 3145732
  (61 other events, 2246.7 us)
Sparse Core Ops, SparseCore 0:
  10.3 313.0 all-gather.16
  325.7 311.9 all-gather.20
  639.9 55.3 all-gather.18
  697.4 51.8 all-gather.28
  751.4 298.5 all-gather.30
  1051.4 45.9 all-gather.32
  1098.9 46.6 all-gather.22
  1147.9 300.9 all-gather.34
  1451.1 311.9 all-gather.24
  1765.2 312.4 all-gather.26
  2157.3 43.9 reduce-scatter.15
  2203.5 41.5 reduce-scatter.17
  2257.8 54.3 reduce-scatter.13
  2314.5 51.9 reduce-scatter.11
  2368.7 642.0 reduce-scatter.21
  3013.1 638.8 reduce-scatter.19
  3657.9 132.9 all-reduce.11
  3797.7 288.1 all-reduce.13
  4088.9 668.4 reduce-scatter.25
  4760.3 665.3 reduce-scatter.23
where the time goes:
time: 5440 us; the launch traced here: 5430 us
  waiting for transfers between devices  3930 us (72%)
  blocking collectives  1050 us (19%)
  matrix products  189 us (3%)
  local copies, waits for them, and re-layouts  177 us (3%)
  other arithmetic  71.7 us (1%)
    reduce_scatter x1, waiting for transfers between devices, local(): lax.psum_scatter(grad_down, ('fsdp', 'seq'), scatter_dimension=0, tiled=T...  669 us
    reduce_scatter x1, waiting for transfers between devices, local(): lax.psum_scatter(grad_up, ('fsdp', 'seq'), scatter_dimension=0, tiled=True)  668 us
    reduce_scatter x1, waiting for transfers between devices, local(): lax.psum_scatter(grad_self_mix, ('fsdp', 'seq'), scatter_dimension=0, til...  641 us
    reduce_scatter x1, waiting for transfers between devices, local(): lax.psum_scatter(grad_cross_mix, ('fsdp', 'seq'), scatter_dimension=0, ti...  583 us
    unnamed x22, waiting for transfers between devices  427 us
    all_gather x1, blocking collectives, local(): lax.all_gather(self_small, ('fsdp', 'seq'), axis=1, tiled=True)  319 us
    all_gather x1, blocking collectives, local(): lax.all_gather(cross_small, ('fsdp', 'seq'), axis=1, tiled=True)  319 us
    all_gather x1, blocking collectives, local(): lax.all_gather(ffn_small, ('fsdp', 'seq'), axis=1, tiled=True)  313 us
  transfers between devices with their start and end apart: 20, of which 10 were waited for; matrix products, arithmetic and copies ran while one was open for 6% of the time, Pallas kernels for 0%

commit v1 on v0

v1 whole, which is shorter than its diff:
```python
import functools

import jax
import jax.numpy as jnp
from jax import lax
from jax.experimental import pallas as pl
from jax.experimental.pallas import tpu as pltpu
from jax.sharding import Mesh
from jax.sharding import PartitionSpec as P

D = 1024
FF = 4096
GROUPS = 8
LANES = 128
HALF = 64
BLOCK = 256
EPS = 1e-05
MASKED = -1e30

SEQ = ("yl", "z")
CHIPS = ("yh", "x", "yl", "z")
PLANE = ("yh", "yl", "x")
BF = jnp.bfloat16
F32 = jnp.float32


def dot(a, b):
    return jnp.dot(a, b, preferred_element_type=F32)


def dot_nt(a, b):
    return lax.dot_general(a, b, (((1,), (1,)), ((), ())), preferred_element_type=F32)


def dot_tn(a, b):
    return lax.dot_general(a, b, (((0,), (0,)), ((), ())), preferred_element_type=F32)


def stack_cols(xt):
    zero = jnp.zeros((HALF, xt.shape[1]), xt.dtype)
    return jnp.concatenate(
        [
            jnp.concatenate([xt[:HALF], zero], axis=0),
            jnp.concatenate([zero, xt[HALF:]], axis=0),
        ],
        axis=1,
    )


def stack_rows(x):
    lane = lax.broadcasted_iota(jnp.int32, x.shape, 1)
    zero = jnp.zeros_like(x)
    return jnp.concatenate(
        [jnp.where(lane < HALF, x, zero), jnp.where(lane < HALF, zero, x)], axis=0
    )


def unstack_cols(xt):
    n = xt.shape[1] // 2
    return jnp.concatenate([xt[:HALF, :n], xt[HALF:, n:]], axis=0)


def allowed_mask(j, start, length):
    pos = lax.broadcasted_iota(jnp.int32, (BLOCK, start.shape[1]), 0) + j * BLOCK
    off = pos - start
    return (off >= 0) & (off < length)


def attn_fwd_kernel(lo_ref, hi_ref, start_ref, len_ref, q_ref, k_ref, v_ref, o_ref, lse_ref,
                    vt_scr, s_scr, o_scr):
    i = pl.program_id(0)
    nk = vt_scr.shape[0]
    per = BLOCK // k_ref.shape[1]

    @pl.when(i == 0)
    def _():
        for j in range(nk):
            vt_scr[j] = v_ref[j * per:(j + 1) * per].reshape(BLOCK, LANES).astype(F32).T

    q = q_ref[0] * jnp.asarray(0.125, BF)
    qst = stack_cols(q.T)
    start = jnp.concatenate([start_ref[0], start_ref[0]], axis=1)
    length = jnp.concatenate([len_ref[0], len_ref[0]], axis=1)
    lo, hi = lo_ref[i], hi_ref[i]
    width = 2 * BLOCK

    def first(j, m8):
        k = k_ref[pl.ds(j * per, per)].reshape(BLOCK, LANES)
        s = dot(k, qst)
        s = jnp.where(allowed_mask(j, start, length), s, MASKED)
        s_scr[pl.ds(pl.multiple_of(j * BLOCK, BLOCK), BLOCK)] = s
        return jnp.maximum(m8, jnp.max(s.reshape(BLOCK // 8, 8, width), axis=0))

    m8 = lax.fori_loop(lo, hi, first, jnp.full((8, width), MASKED, F32))
    m = jnp.max(m8, axis=0, keepdims=True)
    o_scr[...] = jnp.zeros_like(o_scr)

    def second(j, l8):
        p = jnp.exp(s_scr[pl.ds(pl.multiple_of(j * BLOCK, BLOCK), BLOCK)] - m)
        o_scr[...] += dot(vt_scr[j].astype(BF), p.astype(BF))
        return l8 + jnp.sum(p.reshape(BLOCK // 8, 8, width), axis=0)

    l8 = lax.fori_loop(lo, hi, second, jnp.zeros((8, width), F32))
    l = jnp.sum(l8, axis=0, keepdims=True)
    lse_ref[0] = m + jnp.log(l)
    ot = unstack_cols(o_scr[...] * (1.0 / l))
    o_ref[0] = ot.T.astype(BF)


def attn_bwd_kernel(wide, lo_ref, hi_ref, start_ref, len_ref, lse_ref, q_ref, k_ref, v_ref, o_ref,
                    do_ref, out_ref, kt_scr, dq_scr, dk_scr, dv_scr):
    i = pl.program_id(0)
    nk = kt_scr.shape[0]
    kb = k_ref.shape[1]
    per = BLOCK // kb

    @pl.when(i == 0)
    def _():
        for j in range(nk):
            kt_scr[j] = k_ref[j * per:(j + 1) * per].reshape(BLOCK, LANES).astype(F32).T
        dk_scr[...] = jnp.zeros_like(dk_scr)
        dv_scr[...] = jnp.zeros_like(dv_scr)

    q = q_ref[0] * jnp.asarray(0.125, BF)
    do = do_ref[0]
    qs, qst = stack_rows(q), stack_cols(q.T)
    dot_t = do.T
    dos, dost = stack_rows(do), stack_cols(dot_t)
    prod = dot_t.astype(F32) * o_ref[0].T.astype(F32)
    delta = jnp.concatenate(
        [
            jnp.sum(prod[:HALF], axis=0, keepdims=True),
            jnp.sum(prod[HALF:], axis=0, keepdims=True),
        ],
        axis=1,
    )
    lse = lse_ref[0]
    start = jnp.concatenate([start_ref[0], start_ref[0]], axis=1)
    length = jnp.concatenate([len_ref[0], len_ref[0]], axis=1)
    dq_scr[...] = jnp.zeros_like(dq_scr)

    def body(j, carry):
        k = k_ref[pl.ds(j * per, per)].reshape(BLOCK, LANES)
        v = v_ref[pl.ds(j * per, per)].reshape(BLOCK, LANES)
        s = jnp.where(allowed_mask(j, start, length), dot(k, qst), MASKED)
        p = jnp.exp(s - lse)
        ds = (p * (dot(v, dost) - delta)).astype(BF)
        rows = pl.ds(pl.multiple_of(j * BLOCK, BLOCK), BLOCK)
        dv_scr[rows] += dot(p.astype(BF), dos)
        dk_scr[rows] += dot(ds, qs)
        dq_scr[...] += dot(kt_scr[j].astype(BF), ds)
        return carry

    lax.fori_loop(lo_ref[i], hi_ref[i], body, 0)
    dq = (unstack_cols(dq_scr[...]) * 0.125).T.astype(BF)
    if wide:
        out_ref[i, :, :LANES] = dq
    else:
        out_ref[i, :BLOCK] = dq

    @pl.when(i == pl.num_programs(0) - 1)
    def _():
        n = GROUPS
        dk = dk_scr[...].astype(BF).reshape(n, kb, LANES)
        dv = dv_scr[...].astype(BF).reshape(n, kb, LANES)
        if wide:
            out_ref[:, :, LANES:2 * LANES] = dk
            out_ref[:, :, 2 * LANES:] = dv
        else:
            out_ref[:, BLOCK:BLOCK + kb] = dk
            out_ref[:, BLOCK + kb:] = dv


def row_spec(n):
    return pl.BlockSpec((1, 1, n), lambda i, lo, hi: (i, 0, 0))


def block_rows():
    return pl.BlockSpec((1, BLOCK, LANES), lambda i, lo, hi: (i, 0, 0))


def key_specs(kshape, kblock, vblock):
    return [
        pl.BlockSpec(kshape, lambda i, lo, hi: kblock),
        pl.BlockSpec(kshape, lambda i, lo, hi: vblock),
    ]


def attend_fwd(plan, q, kv, keys_at):
    lo, hi, start, length = plan
    nq = lo.shape[0]
    keys = keys_at[0][0] * keys_at[0][1]
    return pl.pallas_call(
        attn_fwd_kernel,
        grid_spec=pltpu.PrefetchScalarGridSpec(
            num_scalar_prefetch=2,
            grid=(nq,),
            in_specs=[row_spec(BLOCK), row_spec(BLOCK), block_rows()] + key_specs(*keys_at),
            out_specs=[block_rows(), row_spec(2 * BLOCK)],
            scratch_shapes=[
                pltpu.VMEM((keys // BLOCK, LANES, BLOCK), F32),
                pltpu.VMEM((keys, 2 * BLOCK), F32),
                pltpu.VMEM((LANES, 2 * BLOCK), F32),
            ],
        ),
        out_shape=[
            jax.ShapeDtypeStruct((nq, BLOCK, LANES), BF),
            jax.ShapeDtypeStruct((nq, 1, 2 * BLOCK), F32),
        ],
        compiler_params=params(),
        cost_estimate=cost(8e9, 4e6),
    )(lo, hi, start, length, q, kv, kv)


def attend_bwd(plan, lse, q, kv, out, grad, keys_at, wide):
    lo, hi, start, length = plan
    nq = lo.shape[0]
    keys = keys_at[0][0] * keys_at[0][1]
    shape = (nq, BLOCK, 3 * LANES) if wide else (nq, BLOCK + 2 * keys_at[0][1], LANES)
    return pl.pallas_call(
        functools.partial(attn_bwd_kernel, wide),
        grid_spec=pltpu.PrefetchScalarGridSpec(
            num_scalar_prefetch=2,
            grid=(nq,),
            in_specs=[row_spec(BLOCK), row_spec(BLOCK), row_spec(2 * BLOCK), block_rows()]
            + key_specs(*keys_at)
            + [block_rows(), block_rows()],
            out_specs=pl.BlockSpec(shape, lambda i, lo, hi: (0, 0, 0)),
            scratch_shapes=[
                pltpu.VMEM((keys // BLOCK, LANES, BLOCK), F32),
                pltpu.VMEM((LANES, 2 * BLOCK), F32),
                pltpu.VMEM((keys, LANES), F32),
                pltpu.VMEM((keys, LANES), F32),
            ],
        ),
        out_shape=jax.ShapeDtypeStruct(shape, BF),
        compiler_params=params(),
        cost_estimate=cost(8e9, 6e6),
    )(lo, hi, start, length, lse, q, kv, kv, out, grad)


def key_plan(query_ids, key_ids, causal):
    start = jnp.sum((key_ids[None, :] < query_ids[:, None]).astype(jnp.int32), axis=1)
    if causal:
        end = jnp.arange(query_ids.shape[0], dtype=jnp.int32) + 1
    else:
        end = jnp.sum((key_ids[None, :] <= query_ids[:, None]).astype(jnp.int32), axis=1)
    start = start.reshape(-1, 1, BLOCK)
    end = end.reshape(-1, 1, BLOCK)
    lo = jnp.min(start, axis=(1, 2)) // BLOCK
    hi = (jnp.max(end, axis=(1, 2)) + BLOCK - 1) // BLOCK
    return lo, hi, start, end - start


def params():
    return pltpu.CompilerParams(vmem_limit_bytes=44 * 2**20)


def cost(flops, size):
    return pl.CostEstimate(flops=int(flops), bytes_accessed=int(size), transcendentals=0)


def norm_forward(values, gain, shift):
    centered = values - jnp.mean(values, axis=-1, keepdims=True)
    inverse = lax.rsqrt(jnp.mean(centered * centered, axis=-1, keepdims=True) + EPS)
    normed = centered * inverse
    return normed * gain + shift, normed, inverse


def column_sum(x):
    return jnp.sum(x, axis=0, keepdims=True)


def norm_backward(upstream, normed, inverse, gain):
    scaled = upstream * gain
    inner = (
        scaled
        - jnp.mean(scaled, axis=-1, keepdims=True)
        - normed * jnp.mean(scaled * normed, axis=-1, keepdims=True)
    )
    return inverse * inner, column_sum(upstream * normed), column_sum(upstream)


PLACES = tuple(yh * 8 + yl * 4 + x for yh in range(2) for x in range(4) for yl in range(2))


def rows_of(ref):
    return jnp.concatenate([ref[p, 0] for p in PLACES], axis=0)


def plane_rows(ref):
    return ref[:, 0].reshape(512, ref.shape[3])


def put_rows(ref, value, other=None):
    for i, p in enumerate(PLACES):
        piece = value[i * 32:(i + 1) * 32]
        if other is not None:
            piece = piece + other[p, 0].astype(F32)
        ref[p, 0] = piece.astype(ref.dtype)


def halves(core, x):
    n = x.shape[1] // 2
    a, b = x[:, :n], x[:, n:]
    first = core == 0
    return jnp.where(first, a, b), jnp.where(first, b, a)


def ordered(core, mine, theirs):
    first = core == 0
    return jnp.concatenate(
        [jnp.where(first, mine, theirs), jnp.where(first, theirs, mine)], axis=1
    )


def joined(ref, first=0, count=None):
    count = ref.shape[1] if count is None else count
    return jnp.concatenate([ref[g, first:first + count] for g in range(GROUPS)], axis=1)


def put_groups(ref, value):
    for g in range(GROUPS):
        ref[g] = value[:, g * LANES:(g + 1) * LANES].astype(ref.dtype)


def qkv_kernel(core_ref, x_ref, own_tile_ref, other_tile_ref, own_ref, other_ref,
               qkv_ref, a1_ref, vec_ref):
    g = pl.program_id(0)
    core = core_ref[0]

    @pl.when(g == 0)
    def _():
        own = own_tile_ref[...].astype(F32).T[:16]
        other = other_tile_ref[...].astype(F32).T[:16]
        vec = ordered(core, own, other)
        vec_ref[...] = vec
        a, _, _ = norm_forward(x_ref[...].astype(F32), vec[0:1], vec[4:5])
        mine, theirs = halves(core, a)
        a1_ref[0] = mine.astype(BF)
        a1_ref[1] = theirs.astype(BF)

    y = dot(a1_ref[0], own_ref[...]) + dot(a1_ref[1], other_ref[...])
    at = pl.ds(pl.multiple_of(g * LANES, LANES), LANES)
    bias = jnp.concatenate(
        [vec_ref[8:9, at], jnp.zeros((1, LANES), F32), vec_ref[9:10, at]], axis=1
    )
    qkv_ref[0] = (y + bias).astype(BF)


def text_kernel(core_ref, enc_ref, vec_ref, own_ref, other_ref, out_ref):
    m = pl.program_id(0)
    mine, theirs = halves(core_ref[0], enc_ref[...])
    y = dot(mine, rows_of(own_ref)) + dot(theirs, rows_of(other_ref))
    put_groups(out_ref, y + vec_ref[12:13] * m.astype(F32))


def middle_kernel(core_ref, o1_ref, x_ref, vec_ref, wo_own, wo_other, wq_own, wq_other,
                  x1_ref, a2_ref, q2_ref):
    core = core_ref[0]
    mine, theirs = halves(core, joined(o1_ref))
    x1 = (
        x_ref[...].astype(F32)
        + dot(mine, rows_of(wo_own))
        + dot(theirs, rows_of(wo_other))
        + vec_ref[10:11]
    )
    x1_ref[...] = x1
    a, _, _ = norm_forward(x1, vec_ref[1:2], vec_ref[5:6])
    mine, theirs = halves(core, a)
    mine, theirs = mine.astype(BF), theirs.astype(BF)
    a2_ref[0] = mine
    a2_ref[1] = theirs
    q2 = dot(mine, rows_of(wq_own)) + dot(theirs, rows_of(wq_other)) + vec_ref[11:12]
    put_groups(q2_ref, q2)


def ffn_kernel(core_ref, o2_ref, x1_ref, vec_ref, upb_ref, cot_ref, wo_own, wo_other,
               up_own, up_other, dn_own, dn_other,
               out_ref, g2_ref, e2_ref, do2_ref, a3_ref, e3_ref, hid_ref, ep_ref, small_ref,
               dupb_ref, gup_ref, gdn_ref,
               x2_scr, acc_scr, pre_scr, hid_scr, da_scr, dh_scr, a3t_scr):
    s = pl.program_id(0)
    t = lax.rem(s, 8)
    core = core_ref[0]

    @pl.when(s == 0)
    def _():
        mine, theirs = halves(core, joined(o2_ref))
        x2 = (
            x1_ref[...]
            + dot(mine, rows_of(wo_own))
            + dot(theirs, rows_of(wo_other))
            + vec_ref[13:14]
        )
        x2_scr[...] = x2
        a, _, _ = norm_forward(x2, vec_ref[2:3], vec_ref[6:7])
        mine, theirs = halves(core, a)
        a3_ref[0] = mine.astype(BF)
        a3_ref[1] = theirs.astype(BF)
        acc_scr[...] = jnp.zeros_like(acc_scr)

    @pl.when(s < 8)
    def _():
        pre = dot(a3_ref[0], rows_of(up_own)) + dot(a3_ref[1], rows_of(up_other)) + upb_ref[...]
        pre_scr[t] = pre
        hidden = (pre * jax.nn.sigmoid(pre)).astype(BF)
        hid_scr[t] = hidden

        @pl.when(t < 4)
        def _():
            acc_scr[...] += dot(hidden, plane_rows(dn_own))

        @pl.when(t >= 4)
        def _():
            acc_scr[...] += dot(hidden, plane_rows(dn_other))

    @pl.when(s == 7)
    def _():
        x3 = x2_scr[...] + acc_scr[...] + vec_ref[14:15]
        y, n4, r4 = norm_forward(x3, vec_ref[3:4], vec_ref[7:8])
        out_ref[...] = y
        g3, dgain, dshift = norm_backward(cot_ref[...].astype(F32), n4, r4, vec_ref[3:4])
        acc_scr[...] = g3
        e3_ref[...] = g3.astype(BF)
        small_ref[0:1] = dgain
        small_ref[1:2] = dshift
        small_ref[2:3] = column_sum(g3)
        da_scr[...] = jnp.zeros_like(da_scr)
        a3t_scr[...] = a3_ref[1].astype(F32).T

    @pl.when(s >= 8)
    def _():
        e3 = e3_ref[...]

        @pl.when(t < 4)
        def _():
            dh_scr[...] = dot_nt(e3, plane_rows(dn_own))
            hid_ref[...] = hid_scr[t]

        @pl.when(t >= 4)
        def _():
            dh_scr[...] = dot_nt(e3, plane_rows(dn_other))
            gdn_ref[:, 0] = dot_tn(hid_scr[t], e3).astype(BF).reshape(16, 32, D)

        pre = pre_scr[t]
        sig = jax.nn.sigmoid(pre)
        dpre = dh_scr[...] * sig * (1.0 + pre * (1.0 - sig))
        ep = dpre.astype(BF)
        ep_ref[...] = ep
        dupb_ref[...] = column_sum(dpre)
        put_rows(gup_ref, dot(a3t_scr[...].astype(BF), ep))
        da_scr[0] += dot_nt(ep, rows_of(up_own))
        da_scr[1] += dot_nt(ep, rows_of(up_other))

    @pl.when(s == 15)
    def _():
        da3 = ordered(core, da_scr[0], da_scr[1])
        _, n3, r3 = norm_forward(x2_scr[...], vec_ref[2:3], vec_ref[6:7])
        back, dgain, dshift = norm_backward(da3, n3, r3, vec_ref[2:3])
        g2 = acc_scr[...] + back
        g2_ref[...] = g2
        small_ref[3:4] = dgain
        small_ref[4:5] = dshift
        small_ref[5:6] = column_sum(g2)
        e2 = g2.astype(BF)
        e2_ref[...] = e2
        put_groups(
            do2_ref, ordered(core, dot_nt(e2, rows_of(wo_own)), dot_nt(e2, rows_of(wo_other)))
        )


def ffn_grad_kernel(core_ref, a3_ref, ep_ref, hid_ref, e3_ref, up_ref, dn_ref, out_ref):
    m = pl.program_id(0)

    @pl.when(m < 4)
    def _():
        put_rows(out_ref, dot_tn(a3_ref[0], ep_ref[...]), up_ref)

    @pl.when(m >= 4)
    def _():
        g = dot_tn(hid_ref[...], e3_ref[...]).reshape(16, 32, D)
        out_ref[:, 0] = (g + dn_ref[:, 0].astype(F32)).astype(BF)


def cross_back_kernel(core_ref, b2_ref, x1_ref, g2_ref, vec_ref, wq_own, wq_other,
                      wo_own, wo_other, g1_ref, e1_ref, do1_ref, small_ref):
    core = core_ref[0]
    dq = joined(b2_ref, 0, BLOCK)
    da2 = ordered(core, dot_nt(dq, rows_of(wq_own)), dot_nt(dq, rows_of(wq_other)))
    _, n2, r2 = norm_forward(x1_ref[...], vec_ref[1:2], vec_ref[5:6])
    back, dgain, dshift = norm_backward(da2, n2, r2, vec_ref[1:2])
    g1 = g2_ref[...] + back
    g1_ref[...] = g1
    e1 = g1.astype(BF)
    e1_ref[...] = e1
    put_groups(
        do1_ref, ordered(core, dot_nt(e1, rows_of(wo_own)), dot_nt(e1, rows_of(wo_other)))
    )
    small_ref[0:1] = dgain
    small_ref[1:2] = dshift
    small_ref[2:3] = column_sum(g1)
    small_ref[3:4] = column_sum(dq.astype(F32))
    small_ref[4:5] = column_sum(joined(b2_ref, BLOCK + 128, 128).astype(F32))


def text_back_kernel(core_ref, b2_ref, wk_own, wk_other, wv_own, wv_other, out_ref):
    dk = joined(b2_ref, BLOCK, 128)
    dv = joined(b2_ref, BLOCK + 128, 128)
    mine = dot_nt(dk, rows_of(wk_own)) + dot_nt(dv, rows_of(wv_own))
    theirs = dot_nt(dk, rows_of(wk_other)) + dot_nt(dv, rows_of(wv_other))
    out_ref[...] = ordered(core_ref[0], mine, theirs)


def attn_grad_kernel(half, core_ref, a2_ref, enc_ref, o1_ref, o2_ref, b2_ref, e1_ref, e2_ref,
                     *rest):
    other = rest[0] if len(rest) == 2 else None
    out_ref = rest[-1]
    core = core_ref[0]
    m = pl.program_id(0)

    def emit(at, a, g):
        @pl.when(m == at)
        def _():
            put_rows(out_ref, dot_tn(a(), g()), other)

    emit(0, lambda: a2_ref[half], lambda: joined(b2_ref, 0, BLOCK))
    emit(1, lambda: halves(core, enc_ref[...])[half], lambda: joined(b2_ref, BLOCK, 128))
    emit(2, lambda: halves(core, enc_ref[...])[half], lambda: joined(b2_ref, BLOCK + 128, 128))
    emit(3, lambda: halves(core, joined(o1_ref))[half], lambda: e1_ref[...])
    emit(4, lambda: halves(core, joined(o2_ref))[half], lambda: e2_ref[...])


def self_grad_kernel(a1_ref, d_ref, out_ref):
    a = a1_ref[1]
    for g in range(GROUPS):
        out_ref[:, g * 384:(g + 1) * 384] = dot_tn(a, d_ref[g]).astype(BF)


def self_grad_own_kernel(a1_ref, d_ref, recv_ref, small_ref, small_recv_ref, out_ref):
    a = a1_ref[0]
    for g in range(GROUPS):
        at = slice(g * 384, (g + 1) * 384)
        out_ref[:, at] = (dot_tn(a, d_ref[g]) + recv_ref[:, at].astype(F32)).astype(BF)
    out_ref[:, 3 * D:] = (small_ref[...] + small_recv_ref[...].astype(F32)).astype(BF)


def self_back_kernel(core_ref, d_ref, own_ref, other_ref, x_ref, g1_ref, vec_ref,
                     out_ref, small_ref, sum_ref, da_scr):
    g = pl.program_id(0)

    @pl.when(g == 0)
    def _():
        da_scr[...] = jnp.zeros_like(da_scr)

    d = d_ref[0]
    sum_ref[0] = column_sum(d.astype(F32))
    da_scr[0] += dot_nt(d, own_ref[...])
    da_scr[1] += dot_nt(d, other_ref[...])

    @pl.when(g == pl.num_programs(0) - 1)
    def _():
        da1 = ordered(core_ref[0], da_scr[0], da_scr[1])
        _, n1, r1 = norm_forward(x_ref[...].astype(F32), vec_ref[0:1], vec_ref[4:5])
        back, dgain, dshift = norm_backward(da1, n1, r1, vec_ref[0:1])
        out_ref[...] = g1_ref[...] + back
        small_ref[0:1] = dgain
        small_ref[1:2] = dshift


def whole(shape):
    return pl.BlockSpec(shape, lambda *a: (0,) * len(shape))


def matrix(m):
    return pl.BlockSpec((16, 1, 32, D), lambda *a: (0, m, 0, 0))


def call(kernel, grid, in_specs, out_specs, out_shape, scratch, flops, size):
    return pl.pallas_call(
        kernel,
        grid_spec=pltpu.PrefetchScalarGridSpec(
            num_scalar_prefetch=1,
            grid=grid,
            in_specs=in_specs,
            out_specs=out_specs,
            scratch_shapes=scratch,
        ),
        out_shape=out_shape,
        compiler_params=params(),
        cost_estimate=cost(flops, size),
    )


def shape(dims, dtype=BF):
    return jax.ShapeDtypeStruct(dims, dtype)


def by_core(x):
    lead = x.shape[:-1]
    return x.reshape(*lead, 8, 2, HALF).swapaxes(-3, -2).reshape(*lead, D)


def by_place(x):
    lead = x.shape[:-1]
    return x.reshape(*lead, 2, 8, HALF).swapaxes(-3, -2).reshape(*lead, D)


def swap(x):
    return lax.ppermute(x, "c", [(0, 1), (1, 0)])


def local(
    tokens,
    encoded,
    unit_ids,
    text_ids,
    cotangent,
    attn_in,
    attn_out,
    w_up,
    w_down,
    norm_gains,
    shifts,
    biases,
    up_bias,
):
    core = lax.axis_index("c")
    first_core = core == 0
    core_arg = core.astype(jnp.int32).reshape(1)
    rows = tokens.shape[1]
    text_rows = encoded.shape[1]

    def mine(x):
        return lax.dynamic_slice_in_dim(x, core * (x.shape[0] // 2), x.shape[0] // 2, 0)

    def theirs(x):
        return lax.dynamic_slice_in_dim(x, (1 - core) * (x.shape[0] // 2), x.shape[0] // 2, 0)

    in_low = by_core(attn_in.astype(BF))
    out_low = by_core(attn_out.astype(BF))
    self_cols = (
        in_low[0:3].reshape(3, 8, GROUPS, LANES).transpose(1, 2, 0, 3).reshape(8, 3 * D)
    )
    vectors = jnp.concatenate([norm_gains, shifts, biases], axis=0).astype(BF)
    tile = jnp.concatenate(
        [
            vectors.T,
            up_bias.astype(BF).reshape(8, 4),
            jnp.zeros((8, 13), BF),
            unit_ids.reshape(8, 32).astype(BF),
            text_ids.reshape(8, 16).astype(BF),
            jnp.zeros((8, 48), BF),
        ],
        axis=1,
    )
    first_pack = jnp.concatenate([self_cols, tile], axis=1)
    width = 3 * D + LANES
    first_all = lax.all_to_all(
        jnp.broadcast_to(first_pack[None], (64, 8, width)), CHIPS, 0, 0, tiled=True
    )
    self_own = first_all.reshape(512, width)
    self_other = swap(self_own)

    up_low = w_up.astype(BF).reshape(8, 2, 4, 2, 2, 4, 32).transpose(0, 3, 5, 1, 4, 2, 6)
    up_low = up_low.reshape(8, 4, D).transpose(1, 0, 2).reshape(32, D)
    down_low = by_core(w_down.astype(BF))
    attn_low = jnp.concatenate([in_low[3:6], out_low], axis=0).reshape(40, D)
    z_pack = jnp.concatenate([up_low, down_low, attn_low], axis=0)
    z_all = lax.all_gather(z_pack, "z", axis=0, tiled=False)
    attn_z = z_all[:, 64:].reshape(4, 5, 8, D).transpose(1, 0, 2, 3).reshape(1, 5, 32, D)
    up_z = z_all[:, :32].reshape(4, 4, 8, D).transpose(1, 0, 2, 3).reshape(4, 32, D)
    ffn_z = jnp.concatenate([up_z, z_all[:, 32:64]], axis=0)[None]
    attn_own = lax.all_gather(attn_z, PLANE, axis=0, tiled=True)
    attn_other = swap(attn_own)
    ffn_own = lax.all_gather(ffn_z, PLANE, axis=0, tiled=True)
    ffn_other = swap(ffn_own)

    x = by_core(tokens[0])
    enc = by_core(encoded[0])
    cot = by_core(cotangent[0])

    tile_own, tile_other = self_own[:, 3 * D:], self_other[:, 3 * D:]

    def up_part(t):
        return t[:, 15:19].reshape(2, 4, 2, 4, 32).transpose(3, 0, 2, 1, 4).reshape(1, 2048)

    up_own, up_other = up_part(tile_own), up_part(tile_other)
    up_vec = jnp.concatenate(
        [jnp.where(first_core, up_own, up_other), jnp.where(first_core, up_other, up_own)], axis=1
    ).astype(F32)
    place = lax.axis_index(("yh", "x"))
    seq_tile = lax.dynamic_slice_in_dim(tile_own, place * 64, 64, 0)
    seq_tile = seq_tile.reshape(8, 8, LANES).astype(F32).astype(jnp.int32)
    units = seq_tile[:, :, 32:64].reshape(-1)
    texts = seq_tile[:, :, 64:80].reshape(-1)
    self_plan = key_plan(units, units, True)
    cross_plan = key_plan(units, texts, False)

    qkv, a1, vec = call(
        qkv_kernel,
        (GROUPS,),
        [
            whole((rows, D)),
            pl.BlockSpec((512, LANES), lambda g, c: (0, 24)),
            pl.BlockSpec((512, LANES), lambda g, c: (0, 24)),
            pl.BlockSpec((512, 384), lambda g, c: (0, g)),
            pl.BlockSpec((512, 384), lambda g, c: (0, g)),
        ],
        [
            pl.BlockSpec((1, rows, 384), lambda g, c: (g, 0, 0)),
            whole((2, rows, 512)),
            whole((16, D)),
        ],
        [shape((GROUPS, rows, 384)), shape((2, rows, 512)), shape((16, D), F32)],
        [],
        1.6e9,
        8e6,
    )(core_arg, x, self_own, self_other, self_own, self_other)
    qkv = lax.all_to_all(qkv, SEQ, 0, 0, tiled=True)
    self_keys = ((GROUPS, rows, LANES), (0, 0, 1), (0, 0, 2))
    o1_heads, lse1 = attend_fwd(self_plan, qkv, qkv, self_keys)
    o1 = lax.all_to_all(o1_heads, SEQ, 0, 0, tiled=True)

    kv2 = call(
        text_kernel,
        (2,),
        [
            whole((text_rows, D)),
            whole((16, D)),
            pl.BlockSpec((16, 1, 32, D), lambda m, c: (0, 1 + m, 0, 0)),
            pl.BlockSpec((16, 1, 32, D), lambda m, c: (0, 1 + m, 0, 0)),
        ],
        pl.BlockSpec((GROUPS, text_rows, LANES), lambda m, c: (0, m, 0)),
        shape((GROUPS, 2 * text_rows, LANES)),
        [],
        0.5e9,
        4e6,
    )(core_arg, enc, vec, attn_own, attn_other)
    kv2 = lax.all_to_all(kv2, SEQ, 0, 0, tiled=True)

    x1, a2, q2 = call(
        middle_kernel,
        (1,),
        [whole((GROUPS, rows, LANES)), whole((rows, D)), whole((16, D))]
        + [matrix(3), matrix(3), matrix(0), matrix(0)],
        [whole((rows, D)), whole((2, rows, 512)), whole((GROUPS, rows, LANES))],
        [shape((rows, D), F32), shape((2, rows, 512)), shape((GROUPS, rows, LANES))],
        [],
        1.1e9,
        8e6,
    )(core_arg, o1, x, vec, attn_own, attn_other, attn_own, attn_other)
    q2 = lax.all_to_all(q2, SEQ, 0, 0, tiled=True)
    cross_keys = ((GROUPS, text_rows, LANES), (0, 0, 0), (0, 1, 0))
    o2_heads, lse2 = attend_fwd(cross_plan, q2, kv2, cross_keys)
    o2 = lax.all_to_all(o2_heads, SEQ, 0, 0, tiled=True)

    def block_of(s, c):
        t = lax.rem(s, 8)
        return jnp.where(t < 4, c[0], 1 - c[0]) * 4 + lax.rem(t, 4)

    def back_block(s, c):
        return block_of(jnp.maximum(s, 8), c)

    up_spec = pl.BlockSpec(
        (16, 1, 32, 512), lambda s, c: (0, block_of(s, c) // 2, 0, lax.rem(block_of(s, c), 2))
    )
    gup_spec = pl.BlockSpec(
        (16, 1, 32, 512), lambda s, c: (0, back_block(s, c) // 2, 0, lax.rem(back_block(s, c), 2))
    )
    (layer_out, g2, e2, do2, a3, e3, hidden, ep, small_f, dup_bias, gup, gdn) = call(
        ffn_kernel,
        (16,),
        [
            whole((GROUPS, rows, LANES)),
            whole((rows, D)),
            whole((16, D)),
            pl.BlockSpec((1, 512), lambda s, c: (0, block_of(s, c))),
            whole((rows, D)),
            matrix(4),
            matrix(4),
            up_spec,
            up_spec,
            pl.BlockSpec(
                (16, 1, 32, D), lambda s, c: (0, 4 + jnp.minimum(lax.rem(s, 8), 3), 0, 0)
            ),
            pl.BlockSpec(
                (16, 1, 32, D), lambda s, c: (0, jnp.maximum(lax.rem(s, 8), 4), 0, 0)
            ),
        ],
        [
            whole((rows, D)),
            whole((rows, D)),
            whole((rows, D)),
            whole((GROUPS, rows, LANES)),
            whole((2, rows, 512)),
            whole((rows, D)),
            pl.BlockSpec((rows, 512), lambda s, c: (0, jnp.clip(s - 8, 0, 3))),
            pl.BlockSpec((rows, 512), lambda s, c: (0, back_block(s, c))),
            whole((8, D)),
            pl.BlockSpec((1, 512), lambda s, c: (0, back_block(s, c))),
            gup_spec,
            pl.BlockSpec((16, 1, 32, D), lambda s, c: (0, jnp.maximum(s - 12, 0), 0, 0)),
        ],
        [
            shape((rows, D), F32),
            shape((rows, D), F32),
            shape((rows, D)),
            shape((GROUPS, rows, LANES)),
            shape((2, rows, 512)),
            shape((rows, D)),
            shape((rows, FF // 2)),
            shape((rows, FF)),
            shape((8, D), F32),
            shape((1, FF), F32),
            shape((16, 4, 32, D)),
            shape((16, 4, 32, D)),
        ],
        [
            pltpu.VMEM((rows, D), F32),
            pltpu.VMEM((rows, D), F32),
            pltpu.VMEM((8, rows, 512), F32),
            pltpu.VMEM((8, rows, 512), BF),
            pltpu.VMEM((2, rows, 512), F32),
            pltpu.VMEM((rows, 512), F32),
            pltpu.VMEM((512, rows), F32),
        ],
        16e9,
        50e6,
    )(core_arg, o2, x1, vec, up_vec, cot, attn_own, attn_other, ffn_own, ffn_other,
      ffn_own, ffn_other)
    do2 = lax.all_to_all(do2, SEQ, 0, 0, tiled=True)
    gup_recv, gdn_recv = swap(gup), swap(gdn)

    back2 = attend_bwd(cross_plan, lse2, q2, kv2, o2_heads, do2, cross_keys, False)
    back2 = lax.all_to_all(back2, SEQ, 0, 0, tiled=True)
    ffn_grad = call(
        ffn_grad_kernel,
        (8,),
        [
            whole((2, rows, 512)),
            pl.BlockSpec((rows, D), lambda m, c: (0, jnp.minimum(m, 3))),
            pl.BlockSpec((rows, 512), lambda m, c: (0, jnp.maximum(m - 4, 0))),
            whole((rows, D)),
            pl.BlockSpec((16, 1, 32, D), lambda m, c: (0, jnp.minimum(m, 3), 0, 0)),
            pl.BlockSpec((16, 1, 32, D), lambda m, c: (0, jnp.maximum(m - 4, 0), 0, 0)),
        ],
        pl.BlockSpec((16, 1, 32, D), lambda m, c: (0, m, 0, 0)),
        shape((16, 8, 32, D)),
        [],
        2.2e9,
        20e6,
    )(core_arg, a3, ep, hidden, e3, gup_recv, gdn_recv)
    ffn_grad = lax.psum_scatter(
        ffn_grad.reshape(4096, D), PLANE, scatter_dimension=0, tiled=True
    ).reshape(1, 8, 32, D)

    g1, e1, do1, small_c = call(
        cross_back_kernel,
        (1,),
        [whole((GROUPS, rows + 2 * text_rows, LANES)), whole((rows, D)), whole((rows, D))]
        + [whole((16, D)), matrix(0), matrix(0), matrix(3), matrix(3)],
        [whole((rows, D)), whole((rows, D)), whole((GROUPS, rows, LANES)), whole((8, D))],
        [
            shape((rows, D), F32),
            shape((rows, D)),
            shape((GROUPS, rows, LANES)),
            shape((8, D), F32),
        ],
        [],
        1.1e9,
        10e6,
    )(core_arg, back2, x1, g2, vec, attn_own, attn_other, attn_own, attn_other)
    do1 = lax.all_to_all(do1, SEQ, 0, 0, tiled=True)
    d_enc = call(
        text_back_kernel,
        (1,),
        [whole((GROUPS, rows + 2 * text_rows, LANES))]
        + [matrix(1), matrix(1), matrix(2), matrix(2)],
        whole((text_rows, D)),
        shape((text_rows, D), F32),
        [],
        0.5e9,
        5e6,
    )(core_arg, back2, attn_own, attn_other, attn_own, attn_other)

    def attn_grads(half, recv):
        specs = [
            whole((2, rows, 512)),
            whole((text_rows, D)),
            whole((GROUPS, rows, LANES)),
            whole((GROUPS, rows, LANES)),
            whole((GROUPS, rows + 2 * text_rows, LANES)),
            whole((rows, D)),
            whole((rows, D)),
        ]
        block = pl.BlockSpec((16, 1, 32, D), lambda m, c: (0, m, 0, 0))
        return call(
            functools.partial(attn_grad_kernel, half),
            (5,),
            specs + [block] * len(recv),
            block,
            shape((16, 5, 32, D)),
            [],
            1.1e9,
            8e6,
        )(core_arg, a2, enc, o1, o2, back2, e1, e2, *recv)

    attn_grad = attn_grads(0, [swap(attn_grads(1, []))])
    attn_grad = lax.psum_scatter(
        attn_grad.reshape(2560, D), PLANE, scatter_dimension=0, tiled=True
    ).reshape(1, 5, 32, D)

    dqkv = attend_bwd(self_plan, lse1, qkv, qkv, o1_heads, do1, self_keys, True)
    dqkv = lax.all_to_all(dqkv, SEQ, 0, 0, tiled=True)

    def plain(kernel, out, *args):
        return pl.pallas_call(
            kernel, out_shape=out, compiler_params=params(), cost_estimate=cost(0.8e9, 6e6)
        )(*args)

    self_recv = swap(plain(self_grad_kernel, shape((512, 3 * D)), a1, dqkv))
    d_tokens, small_s, dsum = call(
        self_back_kernel,
        (GROUPS,),
        [
            pl.BlockSpec((1, rows, 384), lambda g, c: (g, 0, 0)),
            pl.BlockSpec((512, 384), lambda g, c: (0, g)),
            pl.BlockSpec((512, 384), lambda g, c: (0, g)),
            whole((rows, D)),
            whole((rows, D)),
            whole((16, D)),
        ],
        [
            whole((rows, D)),
            whole((8, D)),
            pl.BlockSpec((1, 1, 384), lambda g, c: (g, 0, 0)),
        ],
        [shape((rows, D), F32), shape((8, D), F32), shape((GROUPS, 1, 384), F32)],
        [pltpu.VMEM((2, rows, 512), F32)],
        1.6e9,
        9e6,
    )(core_arg, dqkv, self_own, self_other, x, g1, vec)

    dsum = dsum.reshape(GROUPS, 3, LANES)
    small = jnp.concatenate(
        [
            small_s[0:1],
            small_c[0:1],
            small_f[3:4],
            small_f[0:1],
            small_s[1:2],
            small_c[1:2],
            small_f[4:5],
            small_f[1:2],
            dsum[:, 0].reshape(1, D),
            dsum[:, 2].reshape(1, D),
            small_c[2:3],
            small_c[3:4],
            small_c[4:5],
            small_f[5:6],
            small_f[2:3],
        ],
        axis=0,
    )
    up_sums = dup_bias.reshape(2, 4, 2, 2, 4, 32).transpose(0, 2, 4, 3, 1, 5).reshape(D, 4)
    small = jnp.concatenate([small.T, up_sums, jnp.zeros((D, LANES - 19), F32)], axis=1)
    small_recv = swap(theirs(small).astype(BF))
    last = plain(
        self_grad_own_kernel, shape((512, width)), a1, dqkv, self_recv, mine(small), small_recv
    )
    last = lax.all_to_all(last.reshape(64, 8, width), CHIPS, 0, 0, tiled=True)
    last = jnp.sum(last.astype(F32), axis=0)

    ffn_grad, attn_grad = ffn_grad[0], attn_grad[0]
    z_grad = jnp.concatenate(
        [
            ffn_grad[:4].reshape(4, 4, 8, D).transpose(1, 0, 2, 3).reshape(4, 32, D),
            ffn_grad[4:],
            attn_grad.reshape(5, 4, 8, D).transpose(1, 0, 2, 3).reshape(4, 40, D),
        ],
        axis=1,
    )
    z_grad = lax.all_to_all(z_grad, "z", 0, 0, tiled=True)
    z_grad = jnp.sum(z_grad.astype(F32), axis=0)
    d_up = z_grad[:32].reshape(4, 8, D).transpose(1, 0, 2).reshape(8, 2, 4, 2, 2, 4, 32)
    d_up = d_up.transpose(0, 3, 5, 1, 4, 2, 6).reshape(8, FF)
    d_down = by_place(z_grad[32:64])
    attn_grad = z_grad[64:].reshape(5, 8, D)
    d_self = last[:, :3 * D].reshape(8, GROUPS, 3, LANES).transpose(2, 0, 1, 3).reshape(3, 8, D)
    d_in = by_place(jnp.concatenate([d_self, attn_grad[:3]], axis=0))
    d_out = by_place(attn_grad[3:])
    d_vec = last[:, 3 * D:3 * D + 15].T
    d_up_bias = last[:, 3 * D + 15:3 * D + 19].reshape(32)
    return (
        by_place(layer_out)[None],
        by_place(d_tokens)[None],
        by_place(d_enc)[None],
        d_in,
        d_out,
        d_up,
        d_down,
        d_vec[0:4],
        d_vec[4:8],
        d_vec[8:15],
        d_up_bias,
    )


def solution(mesh):
    fine = Mesh(mesh.devices.reshape(2, 4, 2, 2, 4), ("yh", "x", "c", "yl", "z"))
    fsdp = ("yh", "x", "c")
    every = fsdp + SEQ
    placed = (
        P(fsdp, SEQ, None),
        P(fsdp, SEQ, None),
        P(fsdp, SEQ),
        P(fsdp, SEQ),
        P(fsdp, SEQ, None),
        P(None, every, None),
        P(None, every, None),
        P(every, None),
        P(every, None),
        P(None, every),
        P(None, every),
        P(None, every),
        P(every),
    )
    return jax.shard_map(
        local,
        mesh=fine,
        in_specs=placed,
        out_specs=(
            P(fsdp, SEQ, None),
            P(fsdp, SEQ, None),
            P(fsdp, SEQ, None),
            P(None, every, None),
            P(None, every, None),
            P(every, None),
            P(every, None),
            P(None, every),
            P(None, every),
            P(None, every),
            P(every),
        ),
        check_vma=False,
    )
```

time: 5440 us -> 685 us (0.13)
  waiting for transfers between devices: 3930 us -> 212 us
  blocking collectives: 1050 us -> 166 us
  matrix products: 189 us -> 0 us
  Pallas kernels: 0 us -> 137 us
  local copies, waits for them, and re-layouts: 177 us -> 89 us
    reduce_scatter x8 -> x2, waiting for transfers between devices: 2610 us -> 59.2 us  [the longest x1 59.2 us: local(): lax.psum_scatter(ffn_grad.reshape(4096, D), PLANE, scatter_dimension=0, t...]
    all_gather x5 -> x1, blocking collectives: 984 us -> 15.1 us  [local(): z_all = lax.all_gather(z_pack, 'z', axis=0, tiled=False)]
    all_gather x10 -> x2, waiting for transfers between devices: 896 us -> 99.6 us  [the longest x1 58.7 us: local(): attn_own = lax.all_gather(attn_z, PLANE, axis=0, tiled=True)]
    unnamed x22 -> x4, waiting for transfers between devices: 427 us -> 0.07 us
    dot_general x77 -> x0, matrix products: 189 us -> none  [the longest x8 19.9 us: one_group(): jnp.einsum('qhd,khd->hqk', g_heads, v_heads, preferred_element_type=jnp.f...]
    all_to_all x0 -> x6, blocking collectives: none -> 151 us  [the longest x1 58.1 us: local(): lax.all_to_all(jnp.broadcast_to(first_pack[None], (64, 8, width)), CHIPS,...]
    pallas_call x0 -> x16, Pallas kernels: none -> 137 us  [the longest x1 31.2 us: local(): call(ffn_kernel, (16,), [whole((GROUPS, rows, LANES)), whole((rows, D)),...]
    unnamed x1 -> x0, blocking collectives: 62.6 us -> none
  transfers between devices with their start and end apart: 20 -> 18, of which waited for: 10 -> 11; matrix products, arithmetic and copies ran while one was open for 6% -> 8% of each run, Pallas kernels for 0% -> 12%
where the time goes in v1:
time: 685 us; the launch traced here: 675 us
  waiting for transfers between devices  212 us (31%)
  blocking collectives  166 us (24%)
  Pallas kernels  137 us (20%)
  local copies, waits for them, and re-layouts  89 us (13%)
  starting transfers between devices  34.4 us (5%)
  other arithmetic  20.9 us (3%)
  between operations  15.4 us (2%)
    reduce_scatter x1, waiting for transfers between devices, local(): lax.psum_scatter(ffn_grad.reshape(4096, D), PLANE, scatter_dimension=0, t...  59.2 us
    all_gather x1, waiting for transfers between devices, local(): attn_own = lax.all_gather(attn_z, PLANE, axis=0, tiled=True)  58.7 us
    all_to_all x1, blocking collectives, local(): lax.all_to_all(jnp.broadcast_to(first_pack[None], (64, 8, width)), CHIPS,...  58.1 us
    unnamed x188, local copies, waits for them, and re-layouts  54.9 us
    all_gather x1, waiting for transfers between devices, local(): ffn_own = lax.all_gather(ffn_z, PLANE, axis=0, tiled=True)  40.9 us
    pallas_call x1, Pallas kernels, local(): call(ffn_kernel, (16,), [whole((GROUPS, rows, LANES)), whole((rows, D)),...  31.2 us
    all_to_all x1, blocking collectives, local(): dqkv = lax.all_to_all(dqkv, SEQ, 0, 0, tiled=True)  28 us
    pallas_call x2, Pallas kernels, attend_bwd(): pl.pallas_call(functools.partial(attn_bwd_kernel, wide), grid_spec=pltpu....  27.2 us
  transfers between devices with their start and end apart: 18, of which 11 were waited for; matrix products, arithmetic and copies ran while one was open for 8% of the time, Pallas kernels for 12%

profile of v1, /device:TPU:0, one launch (start us, length us, event | category | flops | bytes accessed | tf_op | source)
XLA Modules:
  0.0 674.9 jit_solution(7949751751141982618)
XLA Ops:
  11.7 15.1 %all-gather = bf16[416,1024]{1,0:T(8,128)(2,1)S(1)} all-gather(bf16[104,1024]{1,0:T(8,128)(2,1)S(1)} %pad_maximum_fusion.2), channel_id=2, replica_groups=mesh['yh'=2,'x'=4,'c'=2,'yl'=2,'z'=4] {'z'}, dimensions={0}, use_global_device_ids=true | all-gather | bytes 1064960 | tf_op jit(solution)/shard_map/all_gather | solution.py:670
  29.8 58.1 %all_to_all.60 = bf16[64,8,3200]{2,1,0:T(8,128)(2,1)S(1)} all-to-all(bf16[64,8,3200]{2,1,0:T(8,128)(2,1)S(1)} %broadcast_in_dim.20), channel_id=1, replica_groups=mesh['yh'=2,'x'=4,'c'=2,'yl'=2,'z'=4] {'yh','x','yl','z'}, dimensions={0} | all-to-all | bytes 6553600 | tf_op jit(solution)/shard_map/all_to_all | solution.py:659
  87.9 40.9 %all-gather.7.cloned.1.call-done = bf16[128,32,1024]{2,1,0:T(8,128)(2,1)} async-done(((bf16[8,32,1024]{2,1,0:T(8,128)(2,1)}), bf16[128,32,1024]{2,1,0:T(8,128)(2,1)}) %all-gather.7.cloned.1.call-update) | async-done | bytes 8388624 | tf_op jit(solution)/shard_map/all_gather | solution.py:676
  128.8 58.7 %all-gather.5.cloned.1.call-done.wo_own.wq_own.own_ref.wk_own.wv_own = bf16[16,5,32,1024]{3,2,1,0:T(8,128)(2,1)} async-done(((bf16[1,5,32,1024]{3,2,1,0:T(8,128)(2,1)}), bf16[16,5,32,1024]{3,2,1,0:T(8,128)(2,1)}) %all-gather.5.cloned.1.call-update) | async-done | bytes 5242896 | tf_op jit(solution)/shard_map/all_gather | solution.py:674
  194.5 7.2 %shard_map.212 = (bf16[8,256,384]{2,1,0:T(8,128)(2,1)S(1)}, bf16[2,256,512]{2,1,0:T(8,128)(2,1)S(1)}, f32[16,1024]{1,0:T(8,128)S(1)}) custom-call(s32[1]{0:T(128)} %bitcast.core_ref, bf16[256,1024]{1,0:T(8,128)(2,1)S(1)} %copy-done.11, bf16[512,3200]{1,0:T(8,128)(2,1)S(1)} %bitcast.124, bf16[512,3200]{1,0:T(8,128)(2,1)} %collective-permute-done.other_tile_ref.other_ref, ...), custom_call_target="tpu_custom_call" | custom-call | flops 1600000000 | bytes 8000000 | tf_op jit(solution)/shard_map/pallas_call | solution.py:700
  203.8 5.3 all-to-all-start.1
  212.2 18.0 %all-to-all-done.1.q_ref.k_ref.v_ref = bf16[8,256,384]{2,1,0:T(8,128)(2,1)} async-done(((bf16[8,256,384]{2,1,0:T(8,128)(2,1)}), bf16[8,256,384]{2,1,0:T(8,128)(2,1)}, u32[]{:S(2)}, u32[]{:S(2)}) %all-to-all-start.1) | async-done | bytes 1572896 | tf_op jit(solution)/shard_map/all_to_all | solution.py:720
  230.3 15.1 %shard_map.213 = (bf16[8,256,128]{2,1,0:T(8,128)(2,1)S(1)}, f32[8,1,512]{2,1,0:T(1,128)S(1)}) custom-call(s32[8]{0:T(128)S(1)} %get-tuple-element.166.lo_ref, s32[8]{0:T(128)S(1)} %get-tuple-element.165.hi_ref, s32[8,1,256]{2,1,0:T(1,128)S(1)} %bitcast.135, s32[8,1,256]{2,1,0:T(1,128)S(1)} %get-tuple-element.159.len_ref, ...), custom_call_target="tpu_custom_call" | custom-call | flops 8000000000 | bytes 4000000 | tf_op jit(solution)/shard_map/pallas_call | solution.py:193
  245.4 13.3 %all_to_all.61.o1_ref = bf16[8,256,128]{2,1,0:T(8,128)(2,1)S(1)} all-to-all(bf16[8,256,128]{2,1,0:T(8,128)(2,1)S(1)} %get-tuple-element.41.o_ref), channel_id=1, replica_groups=mesh['yh'=2,'x'=4,'c'=2,'yl'=2,'z'=4] {'yl','z'}, dimensions={0} | all-to-all | bytes 1048576 | tf_op jit(solution)/shard_map/all_to_all | solution.py:723
  264.7 4.3 all-to-all-start.3
  287.3 5.7 all-to-all-start.4
  299.7 3.9 all-to-all-done.4.k_ref.v_ref
  304.9 10.8 %shard_map.216 = (bf16[8,256,128]{2,1,0:T(8,128)(2,1)S(1)}, f32[8,1,512]{2,1,0:T(1,128)S(1)}) custom-call(s32[8]{0:T(128)S(1)} %copy-done.68, s32[8]{0:T(128)S(1)} %copy-done.66, s32[8,1,256]{2,1,0:T(1,128)S(1)} %bitcast.132, s32[8,1,256]{2,1,0:T(1,128)S(1)} %get-tuple-element.161.len_ref, bf16[8,256,128]{2,1,0:T(8,128)(2,1)} %all-to-all-done.3.q_ref, ...), custom_call_target="tpu_custom_call" | custom-call | flops 8000000000 | bytes 4000000 | tf_op jit(solution)/shard_map/pallas_call | solution.py:193
  317.2 4.1 all-to-all-start.5
  335.7 31.2 %shard_map.217 = (f32[256,1024]{1,0:T(8,128)S(1)}, f32[256,1024]{1,0:T(8,128)S(1)}, bf16[256,1024]{1,0:T(8,128)(2,1)S(1)}, bf16[8,256,128]{2,1,0:T(8,128)(2,1)S(...) custom-call(s32[1]{0:T(128)} %bitcast.core_ref, ...), custom_call_target="tpu_custom_call" | custom-call | flops 16000000000 | bytes 50000000 | tf_op jit(solution)/shard_map/pallas_call | solution.py:771
  369.3 14.1 %all_to_all.62.do_ref = bf16[8,256,128]{2,1,0:T(8,128)(2,1)S(1)} all-to-all(bf16[8,256,128]{2,1,0:T(8,128)(2,1)S(1)} %get-tuple-element.49), channel_id=1, replica_groups=mesh['yh'=2,'x'=4,'c'=2,'yl'=2,'z'=4] {'yl','z'}, dimensions={0} | all-to-all | bytes 1048576 | tf_op jit(solution)/shard_map/all_to_all | solution.py:832
  383.4 11.4 %shard_map.218 = bf16[8,512,128]{2,1,0:T(8,128)(2,1)S(1)} custom-call(s32[8]{0:T(128)S(1)} %copy-done.69, s32[8]{0:T(128)S(1)} %copy-done.67, s32[8,1,256]{2,1,0:T(1,128)S(1)} %bitcast.133, s32[8,1,256]{2,1,0:T(1,128)S(1)} %copy-done.57, f32[8,1,512]{2,1,0:T(1,128)S(1)} %copy-done.73, bf16[8,256,128]{2,1,0:T(8,128)(2,1)} %all-to-all-done.3.q_ref, ...), custom_call_target="tpu_custom_call" | custom-call | flops 8000000000 | bytes 6000000 | tf_op jit(solution)/shard_map/pallas_call | solution.py:220
  394.9 19.5 %all_to_all.63.b2_ref = bf16[8,512,128]{2,1,0:T(8,128)(2,1)S(1)} all-to-all(bf16[8,512,128]{2,1,0:T(8,128)(2,1)S(1)} %shard_map.218), channel_id=1, replica_groups=mesh['yh'=2,'x'=4,'c'=2,'yl'=2,'z'=4] {'yl','z'}, dimensions={0} | all-to-all | bytes 2097152 | tf_op jit(solution)/shard_map/all_to_all | solution.py:836
  414.5 4.5 shard_map.219
  424.7 8.6 %collective-permute-done.7.rest_0_ = bf16[16,5,32,1024]{3,2,1,0:T(8,128)(2,1)S(1)} collective-permute-done((bf16[16,5,32,1024]{3,2,1,0:T(8,128)(2,1)S(1)}, bf16[16,5,32,1024]{3,2,1,0:T(8,128)(2,1)S(1)}, u32[]{:S(2)}, u32[]{:S(2)}) %collective-permute-start.7) | collective-permute-done | bytes 5242912 | tf_op jit(solution)/shard_map/ppermute | solution.py:610
  435.7 5.5 shard_map.227
  444.3 6.9 %collective-permute-done.5.up_ref = bf16[16,4,32,1024]{3,2,1,0:T(8,128)(2,1)S(1)} collective-permute-done((bf16[16,4,32,1024]{3,2,1,0:T(8,128)(2,1)}, bf16[16,4,32,1024]{3,2,1,0:T(8,128)(2,1)S(1)}, u32[]{:S(2)}, u32[]{:S(2)}) %collective-permute-start.5) | collective-permute-done | bytes 4194336 | tf_op jit(solution)/shard_map/ppermute | solution.py:610
  451.1 6.0 collective-permute-done.6.dn_ref
  464.0 9.3 %shard_map.225 = bf16[16,8,32,1024]{3,2,1,0:T(8,128)(2,1)} custom-call(s32[1]{0:T(128)} %bitcast.core_ref, bf16[2,256,512]{2,1,0:T(8,128)(2,1)S(1)} %copy-done.39, bf16[256,4096]{1,0:T(8,128)(2,1)S(1)} %copy-done.15, bf16[256,2048]{1,0:T(8,128)(2,1)S(1)} %copy-done.30, bf16[256,1024]{1,0:T(8,128)(2,1)S(1)} %copy-done.41, ...), custom_call_target="tpu_custom_call" | custom-call | flops 2200000000 | bytes 20000000 | tf_op jit(solution)/shard_map/pallas_call | solution.py:837
  473.4 17.9 %all_to_all.64.do_ref = bf16[8,256,128]{2,1,0:T(8,128)(2,1)S(1)} all-to-all(bf16[8,256,128]{2,1,0:T(8,128)(2,1)} %copy-done.45), channel_id=1, replica_groups=mesh['yh'=2,'x'=4,'c'=2,'yl'=2,'z'=4] {'yl','z'}, dimensions={0} | all-to-all | bytes 1048576 | tf_op jit(solution)/shard_map/all_to_all | solution.py:874
  492.4 15.7 %shard_map.220 = bf16[8,256,384]{2,1,0:T(8,128)(2,1)S(1)} custom-call(s32[8]{0:T(128)S(1)} %copy-done.65, s32[8]{0:T(128)S(1)} %copy-done.63, s32[8,1,256]{2,1,0:T(1,128)S(1)} %bitcast.136, s32[8,1,256]{2,1,0:T(1,128)S(1)} %copy-done.61, f32[8,1,512]{2,1,0:T(1,128)S(1)} %copy-done.71, bf16[8,256,384]{2,1,0:T(8,128)(2,1)} %all-to-all-done.1.q_ref.k_ref.v_ref, ...), custom_call_target="tpu_custom_call" | custom-call | flops 8000000000 | bytes 6000000 | tf_op jit(solution)/shard_map/pallas_call | solution.py:220
  508.1 28.0 %all_to_all.65.d_ref = bf16[8,256,384]{2,1,0:T(8,128)(2,1)S(1)} all-to-all(bf16[8,256,384]{2,1,0:T(8,128)(2,1)S(1)} %shard_map.220), channel_id=1, replica_groups=mesh['yh'=2,'x'=4,'c'=2,'yl'=2,'z'=4] {'yl','z'}, dimensions={0} | all-to-all | bytes 3145728 | tf_op jit(solution)/shard_map/all_to_all | solution.py:915
  547.7 7.9 %shard_map.221 = (f32[256,1024]{1,0:T(8,128)S(1)}, f32[8,1024]{1,0:T(8,128)S(1)}, f32[8,1,384]{2,1,0:T(1,128)S(1)}) custom-call(s32[1]{0:T(128)} %bitcast.core_ref, bf16[8,256,384]{2,1,0:T(8,128)(2,1)S(1)} %copy-done.5, bf16[512,3200]{1,0:T(8,128)(2,1)S(1)} %bitcast.128, bf16[512,3200]{1,0:T(8,128)(2,1)} %collective-permute-done.other_tile_ref.other_ref, ...), custom_call_target="tpu_custom_call" | custom-call | flops 1600000000 | bytes 9000000 | tf_op jit(solution)/shard_map/pallas_call | solution.py:923
  564.8 8.7 %all-to-all-start.10 = ((bf16[64,8,3200]{2,1,0:T(8,128)(2,1)}), bf16[64,8,3200]{2,1,0:T(8,128)(2,1)}, u32[]{:S(2)}, u32[]{:S(2)}) async-start(bf16[64,8,3200]{2,1,0:T(8,128)(2,1)} %bitcast.130), calls=%async_computation.10 | async-start | bytes 6553600 | tf_op jit(solution)/shard_map/all_to_all | solution.py:972
  585.0 59.2 %reduce-scatter.3.cloned.1.call-done = bf16[256,1024]{1,0:T(8,128)(2,1)} async-done(((bf16[4096,1024]{1,0:T(8,128)(2,1)}), bf16[256,1024]{1,0:T(8,128)(2,1)}) %reduce-scatter.3.cloned.1.call-update) | async-done | bytes 524304 | tf_op jit(solution)/shard_map/reduce_scatter | solution.py:854
  646.3 4.4 all-to-all-start.11
  656.0 6.5 all-to-all-done.11
  (346 shorter events, 133.5 us)
Async XLA Ops:
  7.2 121.6 %all-gather.7.cloned.1.call-start = ((), (), s32[]{:S(2)}) async-start(), calls=%async_computation.17 | async-start | bytes 8912896 | tf_op jit(solution)/shard_map/all_gather | solution.py:676
  27.7 159.8 %all-gather.5.cloned.1.call-start = ((), (), s32[]{:S(2)}) async-start(), calls=%async_computation.14 | async-start | bytes 5570560 | tf_op jit(solution)/shard_map/all_gather | solution.py:674
  87.9 105.6 %collective-permute-start = (bf16[512,3200]{1,0:T(8,128)(2,1)S(1)}, bf16[512,3200]{1,0:T(8,128)(2,1)}, u32[]{:S(2)}, u32[]{:S(2)}) collective-permute-start(bf16[512,3200]{1,0:T(8,128)(2,1)S(1)} %bitcast.123), channel_id=1, source_target_pairs={{0,8},{8,0},{1,9},{9,1},{2,10},{10,2},{3,11},{11,3},{4,12},{12,4},... | collective-permute-start | bytes 9830408 | tf_op jit(solution)/shard_map/ppermute | solution.py:610
  128.8 203.0 %collective-permute-start.2 = (bf16[16,8,32,1024]{3,2,1,0:T(8,128)(2,1)}, bf16[16,8,32,1024]{3,2,1,0:T(8,128)(2,1)}, u32[]{:S(2)}, u32[]{:S(2)}) collective-permute-start(bf16[16,8,32,1024]{3,2,1,0:T(8,128)(2,1)} %bitcast.179), channel_id=1, source_target_pairs={{0,8},{8,0},{1,9},{9,1},{2,10},{10,2},{3,11},{11,3},{4,12},{12,4},... | collective-permute-start | bytes 25165832 | tf_op jit(solution)/shard_map/ppermute | solution.py:610
  187.5 71.2 %collective-permute-start.1 = (bf16[16,5,32,1024]{3,2,1,0:T(8,128)(2,1)}, bf16[16,5,32,1024]{3,2,1,0:T(8,128)(2,1)}, u32[]{:S(2)}, u32[]{:S(2)}) collective-permute-start(bf16[16,5,32,1024]{3,2,1,0:T(8,128)(2,1)} %all-gather.5.cloned.1.call-done.wo_own.wq_own.own_ref.wk_own.wv_own), channel_id=1, source_target_pairs={{0,8},{8,0},{1,9},{9,1},{2,10},{10,2},{3,11},{11,3},{4,12},{12,4},... | collective-permute-start | bytes 15728648 | tf_op jit(solution)/shard_map/ppermute | solution.py:610
  203.8 54.9 %copy-start.23 = (f32[16,1024]{1,0:T(8,128)}, f32[16,1024]{1,0:T(8,128)S(1)}, u32[]{:S(2)}) copy-start(f32[16,1024]{1,0:T(8,128)S(1)} %get-tuple-element.42.vec_ref) | copy-start | bytes 196612
  203.8 26.5 %all-to-all-start.1 = ((bf16[8,256,384]{2,1,0:T(8,128)(2,1)}), bf16[8,256,384]{2,1,0:T(8,128)(2,1)}, u32[]{:S(2)}, u32[]{:S(2)}) async-start(bf16[8,256,384]{2,1,0:T(8,128)(2,1)} %copy-done.22), calls=%async_computation.1 | async-start | bytes 3145728 | tf_op jit(solution)/shard_map/all_to_all | solution.py:720
  210.2 35.2 %copy-start.79 = (s32[2048]{0:T(1024)}, s32[2048]{0:T(1024)S(1)}, u32[]{:S(2)}) copy-start(s32[2048]{0:T(1024)S(1)} %lt.42) | copy-start | bytes 24580
  212.0 33.4 %copy-start.58 = (s32[2048]{0:T(1024)}, s32[2048]{0:T(1024)S(1)}, u32[]{:S(2)}) copy-start(s32[2048]{0:T(1024)S(1)} %convert_reduce_fusion) | copy-start | bytes 24580
  212.2 33.2 %copy-start.60 = (s32[8,1,256]{2,1,0:T(1,128)}, s32[8,1,256]{2,1,0:T(1,128)S(1)}, u32[]{:S(2)}) copy-start(s32[8,1,256]{2,1,0:T(1,128)S(1)} %get-tuple-element.159.len_ref) | copy-start | bytes 24580
  212.2 33.2 %copy-start.62 = (s32[8]{0:T(128)}, s32[8]{0:T(128)S(1)}, u32[]{:S(2)}) copy-start(s32[8]{0:T(128)S(1)} %get-tuple-element.165.hi_ref) | copy-start | bytes 100
  212.2 33.2 %copy-start.64 = (s32[8]{0:T(128)}, s32[8]{0:T(128)S(1)}, u32[]{:S(2)}) copy-start(s32[8]{0:T(128)S(1)} %get-tuple-element.166.lo_ref) | copy-start | bytes 100
  230.3 28.5 %copy-start.12 = (bf16[256,1024]{1,0:T(8,128)(2,1)S(1)}, bf16[256,1024]{1,0:T(8,128)(2,1)}, u32[]{:S(2)}) copy-start(bf16[256,1024]{1,0:T(8,128)(2,1)} %copy.310.x_ref) | copy-start | bytes 1572868
  264.7 22.6 %all-to-all-start.3 = ((bf16[8,256,128]{2,1,0:T(8,128)(2,1)}), bf16[8,256,128]{2,1,0:T(8,128)(2,1)}, u32[]{:S(2)}, u32[]{:S(2)}) async-start(bf16[8,256,128]{2,1,0:T(8,128)(2,1)} %copy-done.48), calls=%async_computation.3 | async-start | bytes 1048576 | tf_op jit(solution)/shard_map/all_to_all | solution.py:753
  287.3 16.3 %all-to-all-start.4 = ((bf16[8,256,128]{2,1,0:T(8,128)(2,1)}), bf16[8,256,128]{2,1,0:T(8,128)(2,1)}, u32[]{:S(2)}, u32[]{:S(2)}) async-start(bf16[8,256,128]{2,1,0:T(8,128)(2,1)} %copy-done.21), calls=%async_computation.4 | async-start | bytes 1048576 | tf_op jit(solution)/shard_map/all_to_all | solution.py:740
  317.2 14.6 %all-to-all-start.5 = ((bf16[8,256,128]{2,1,0:T(8,128)(2,1)}), bf16[8,256,128]{2,1,0:T(8,128)(2,1)}, u32[]{:S(2)}, u32[]{:S(2)}) async-start(bf16[8,256,128]{2,1,0:T(8,128)(2,1)} %copy-done.46), calls=%async_computation.5 | async-start | bytes 1048576 | tf_op jit(solution)/shard_map/all_to_all | solution.py:756
  321.3 262.7 %reduce-scatter.5.cloned.1.call-start = ((), (), s32[]{:S(2)}) async-start(), calls=%async_computation.16 | async-start | bytes 5570560 | tf_op jit(solution)/shard_map/reduce_scatter | solution.py:910
  335.7 47.7 %copy-start.47 = (bf16[8,256,128]{2,1,0:T(8,128)(2,1)S(1)}, bf16[8,256,128]{2,1,0:T(8,128)(2,1)}, u32[]{:S(2)}) copy-start(bf16[8,256,128]{2,1,0:T(8,128)(2,1)} %copy-done.46) | copy-start | bytes 1572868
  335.7 47.7 %copy-start.55 = (s32[2048]{0:T(1024)S(1)}, s32[2048]{0:T(1024)}, u32[]{:S(2)}) copy-start(s32[2048]{0:T(1024)} %copy-done.54) | copy-start | bytes 24580
  335.7 47.7 %copy-start.57 = (s32[8,1,256]{2,1,0:T(1,128)S(1)}, s32[8,1,256]{2,1,0:T(1,128)}, u32[]{:S(2)}) copy-start(s32[8,1,256]{2,1,0:T(1,128)} %copy-done.56) | copy-start | bytes 24580
  335.7 47.7 %copy-start.67 = (s32[8]{0:T(128)S(1)}, s32[8]{0:T(128)}, u32[]{:S(2)}) copy-start(s32[8]{0:T(128)} %get-tuple-element.167.hi_ref) | copy-start | bytes 100
  335.7 47.7 %copy-start.69 = (s32[8]{0:T(128)S(1)}, s32[8]{0:T(128)}, u32[]{:S(2)}) copy-start(s32[8]{0:T(128)} %get-tuple-element.168.lo_ref) | copy-start | bytes 100
  335.7 47.7 %copy-start.73 = (f32[8,1,512]{2,1,0:T(1,128)S(1)}, f32[8,1,512]{2,1,0:T(1,128)}, u32[]{:S(2)}) copy-start(f32[8,1,512]{2,1,0:T(1,128)} %copy-done.72) | copy-start | bytes 49156
  383.4 31.1 %copy-start.37 = (f32[256,1024]{1,0:T(8,128)S(1)}, f32[256,1024]{1,0:T(8,128)}, u32[]{:S(2)}) copy-start(f32[256,1024]{1,0:T(8,128)} %copy-done.35) | copy-start | bytes 3145732
  424.6 8.7 %collective-permute-start.7 = (bf16[16,5,32,1024]{3,2,1,0:T(8,128)(2,1)S(1)}, bf16[16,5,32,1024]{3,2,1,0:T(8,128)(2,1)S(1)}, u32[]{:S(2)}, u32[]{:S(2)}) collective-permute-start(bf16[16,5,32,1024]{3,2,1,0:T(8,128)(2,1)S(1)} %shard_map.226), channel_id=1, source_target_pairs={{0,8},{8,0},{1,9},{9,1},{2,10},{10,2},{3,11},{11,3},{4,12},{12,4},... | collective-permute-start | bytes 15728648 | tf_op jit(solution)/shard_map/ppermute | solution.py:610
  443.6 200.6 %reduce-scatter.3.cloned.1.call-start = ((), (), s32[]{:S(2)}) async-start(), calls=%async_computation.15 | async-start | bytes 8912896 | tf_op jit(solution)/shard_map/reduce_scatter | solution.py:854
  443.7 7.4 %collective-permute-start.5 = (bf16[16,4,32,1024]{3,2,1,0:T(8,128)(2,1)}, bf16[16,4,32,1024]{3,2,1,0:T(8,128)(2,1)S(1)}, u32[]{:S(2)}, u32[]{:S(2)}) collective-permute-start(bf16[16,4,32,1024]{3,2,1,0:T(8,128)(2,1)} %get-tuple-element.64), channel_id=1, source_target_pairs={{0,8},{8,0},{1,9},{9,1},{2,10},{10,2},{3,11},{11,3},{4,12},{12,4},... | collective-permute-start | bytes 12582920 | tf_op jit(solution)/shard_map/ppermute | solution.py:610
  443.9 13.2 %collective-permute-start.6 = (bf16[16,4,32,1024]{3,2,1,0:T(8,128)(2,1)}, bf16[16,4,32,1024]{3,2,1,0:T(8,128)(2,1)S(1)}, u32[]{:S(2)}, u32[]{:S(2)}) collective-permute-start(bf16[16,4,32,1024]{3,2,1,0:T(8,128)(2,1)} %get-tuple-element.65), channel_id=1, source_target_pairs={{0,8},{8,0},{1,9},{9,1},{2,10},{10,2},{3,11},{11,3},{4,12},{12,4},... | collective-permute-start | bytes 12582920 | tf_op jit(solution)/shard_map/ppermute | solution.py:610
  540.2 19.7 %collective-permute-start.3 = (bf16[512,3072]{1,0:T(8,128)(2,1)}, bf16[512,3072]{1,0:T(8,128)(2,1)}, u32[]{:S(2)}, u32[]{:S(2)}) collective-permute-start(bf16[512,3072]{1,0:T(8,128)(2,1)} %shard_map.223), channel_id=1, source_target_pairs={{0,8},{8,0},{1,9},{9,1},{2,10},{10,2},{3,11},{11,3},{4,12},{12,4},... | collective-permute-start | bytes 9437192 | tf_op jit(solution)/shard_map/ppermute | solution.py:610
  558.5 1.4 collective-permute-start.4
  564.8 81.5 %all-to-all-start.10 = ((bf16[64,8,3200]{2,1,0:T(8,128)(2,1)}), bf16[64,8,3200]{2,1,0:T(8,128)(2,1)}, u32[]{:S(2)}, u32[]{:S(2)}) async-start(bf16[64,8,3200]{2,1,0:T(8,128)(2,1)} %bitcast.130), calls=%async_computation.10 | async-start | bytes 6553600 | tf_op jit(solution)/shard_map/all_to_all | solution.py:972
  646.3 16.2 %all-to-all-start.11 = ((bf16[4,104,1024]{2,1,0:T(8,128)(2,1)}), bf16[4,104,1024]{2,1,0:T(8,128)(2,1)S(1)}, u32[]{:S(2)}, u32[]{:S(2)}) async-start(bf16[4,104,1024]{2,1,0:T(8,128)(2,1)} %pad_maximum_fusion), calls=%async_computation.13 | async-start | bytes 1703936 | tf_op jit(solution)/shard_map/all_to_all | solution.py:984
  (75 other events, 586.8 us)
Sparse Core Ops, SparseCore 0:
  27.9 100.8 all-gather.6
  131.5 55.9 all-gather.4
  443.8 79.6 reduce-scatter.4
  526.7 117.4 reduce-scatter.2
